TPU v7x, 256 devices: a whole 4x4x8 slice. The times are simulated.
256 devices in a mesh: row: 8 (over z_hi, x), col: 32 (over y, z_lo, core).
Axes of the slice: x: 4, y: 4, z: 8 (z_hi: 2, z_lo: 4; z = z_hi * 4 + z_lo), core: 2. Of those that a mesh axis runs over, the one named last changes fastest.
Arguments:
- image: bfloat16 [128, 2048, 96], P('row', 'col'), may hold values from -6 to 6
- kernels: float32 [2, 7, 7, 96], replicated, may hold values from -0.875 to 0.875
- gains: float32 [2, 96], replicated, may hold values from 0.5 to 1.5
- up_weights: bfloat16 [2, 96, 384], replicated, may hold values from -0.625 to 0.625
- down_weights: bfloat16 [2, 384, 96], replicated, may hold values from -0.3125 to 0.3125
- cotangent: bfloat16 [128, 2048, 96], P('row', 'col'), may hold values from -6 to 6
Outputs:
- output: bfloat16 [128, 2048, 96], P('row', 'col')
- grad_image: bfloat16 [128, 2048, 96], P('row', 'col')
- grad_kernels: float32 [2, 7, 7, 96], replicated
- grad_gains: float32 [2, 96], replicated
- grad_up: float32 [2, 96, 384], P(None, 'row', 'col')
- grad_down: float32 [2, 384, 96], P(None, 'col', 'row')
All inputs are finite; a program needn't handle non-finite values.
Results may differ from a plain program's by a relative error of at most 0.029.
Values may be sent and summed in bfloat16 or wider, within the bound.
A program may use at most 64 MiB of HBM per device.

v0:
```python
import math

import jax
import jax.numpy as jnp
from jax import lax
from jax.sharding import PartitionSpec as P

epsilon = 1e-06
inv_sqrt_two = 0.7071067811865476
inv_sqrt_two_pi = 0.3989422804014327


def extended(array, sides, width):
    for axis, dim in sides:
        count, length = (lax.axis_size(axis), array.shape[dim])
        up = [(i, (i + 1) % count) for i in range(count - 1)]
        down = [(j, i) for i, j in up]
        last = lax.slice_in_dim(array, length - width, length, axis=dim)
        first = lax.slice_in_dim(array, 0, width, axis=dim)
        before = lax.ppermute(last, axis, up)
        after = lax.ppermute(first, axis, down)
        array = jnp.concatenate([before, array, after], axis=dim)
    return array


def contract_leading(left, right):
    return lax.dot_general(
        left, right, (((0,), (0,)), ((), ())), preferred_element_type=jnp.float32
    )


def contract_trailing(left, right):
    return lax.dot_general(
        left, right, (((1,), (1,)), ((), ())), preferred_element_type=jnp.float32
    )


def depthwise(padded, kernel, tile_rows, tile_cols):
    padded_f = padded.astype(jnp.float32)
    tap_count = kernel.shape[0]
    accumulated = jnp.zeros((tile_rows, tile_cols, padded.shape[2]), jnp.float32)
    for tap_row in range(tap_count):
        for tap_col in range(tap_count):
            accumulated = (
                accumulated
                + padded_f[tap_row : tap_row + tile_rows, tap_col : tap_col + tile_cols]
                * kernel[tap_row, tap_col]
            )
    return accumulated


def flipped_conv(padded, kernel, tile_rows, tile_cols):
    padded_f = padded.astype(jnp.float32)
    tap_count = kernel.shape[0]
    last_tap = tap_count - 1
    accumulated = jnp.zeros((tile_rows, tile_cols, padded.shape[2]), jnp.float32)
    for tap_row in range(tap_count):
        for tap_col in range(tap_count):
            start_row = last_tap - tap_row
            start_col = last_tap - tap_col
            accumulated = (
                accumulated
                + padded_f[start_row : start_row + tile_rows, start_col : start_col + tile_cols]
                * kernel[tap_row, tap_col]
            )
    return accumulated


def kernel_grad(padded, conv_grad, tile_rows, tile_cols, tap_count):
    padded_f = padded.astype(jnp.float32)
    grad_f = conv_grad.astype(jnp.float32)
    rows_out = []
    for tap_row in range(tap_count):
        entries = []
        for tap_col in range(tap_count):
            entries.append(
                jnp.sum(
                    padded_f[tap_row : tap_row + tile_rows, tap_col : tap_col + tile_cols] * grad_f,
                    axis=(0, 1),
                )
            )
        rows_out.append(jnp.stack(entries))
    return jnp.stack(rows_out)


def normalize(conv_out):
    centred = conv_out - jnp.mean(conv_out, axis=-1, keepdims=True)
    variance = jnp.mean(centred * centred, axis=-1, keepdims=True)
    inverse_std = lax.rsqrt(variance + epsilon)
    return (centred * inverse_std, inverse_std)


def gelu_parts(pre):
    normal_cdf = 0.5 * (1.0 + lax.erf(pre * inv_sqrt_two))
    density = jnp.exp(-0.5 * pre * pre) * inv_sqrt_two_pi
    return (pre * normal_cdf, normal_cdf + pre * density)


def mixing(padded, kernel, gain, up_weight, tile_rows, tile_cols):
    conv_out = depthwise(padded, kernel, tile_rows, tile_cols)
    unit_vals, inverse_std = normalize(conv_out)
    normed = (unit_vals * gain).astype(jnp.bfloat16).reshape(tile_rows * tile_cols, -1)
    pre = jnp.dot(normed, up_weight, preferred_element_type=jnp.float32)
    gelu_value, gelu_slope = gelu_parts(pre)
    return (unit_vals, inverse_std, normed, gelu_value.astype(jnp.bfloat16), gelu_slope)


def backward_rows(
    padded, upstream, saved, kernel, gain, up_weight, down_weight, tile_rows, tile_cols
):
    unit_vals, inverse_std, normed, hidden, gelu_slope = saved
    channels = upstream.shape[2]
    flat_grad = upstream.reshape(tile_rows * tile_cols, channels)
    down_term = contract_leading(hidden, flat_grad)
    hidden_grad = contract_trailing(flat_grad, down_weight)
    pre_grad = (hidden_grad * gelu_slope).astype(jnp.bfloat16)
    up_term = contract_leading(normed, pre_grad)
    normed_grad = contract_trailing(pre_grad, up_weight).reshape(tile_rows, tile_cols, channels)
    gain_term = jnp.sum(normed_grad * unit_vals, axis=(0, 1))
    unit_grad = normed_grad * gain
    conv_grad = inverse_std * (
        unit_grad
        - jnp.mean(unit_grad, axis=-1, keepdims=True)
        - unit_vals * jnp.mean(unit_grad * unit_vals, axis=-1, keepdims=True)
    )
    conv_grad = conv_grad.astype(jnp.bfloat16)
    kernel_term = kernel_grad(padded, conv_grad, tile_rows, tile_cols, kernel.shape[0])
    return (conv_grad, kernel_term, gain_term, up_term, down_term)


def deliver(up_term, down_term):
    up_part, down_part = (
        lax.psum_scatter(
            up_term.astype(jnp.bfloat16), "row", scatter_dimension=0, tiled=True
        ).astype(jnp.float32),
        lax.psum_scatter(
            down_term.astype(jnp.bfloat16), "row", scatter_dimension=1, tiled=True
        ).astype(jnp.float32),
    )
    up_part, down_part = (
        lax.psum_scatter(
            up_part.astype(jnp.bfloat16), "col", scatter_dimension=1, tiled=True
        ).astype(jnp.float32),
        lax.psum_scatter(
            down_part.astype(jnp.bfloat16), "col", scatter_dimension=0, tiled=True
        ).astype(jnp.float32),
    )
    return (up_part, down_part)


def per_device(image, kernels, gains, up_weights, down_weights, cotangent):
    tile_rows, tile_cols, channels = image.shape
    layer_count = kernels.shape[0]
    halo_width = kernels.shape[1] // 2
    pixel_total = tile_rows * tile_cols * lax.axis_size("row") * lax.axis_size("col")
    factor = 1.0 / math.sqrt(pixel_total)
    current = image
    stored = []
    saved_list = []
    for layer_index in range(layer_count):
        padded = extended(current, (("row", 0), ("col", 1)), halo_width)
        stored.append(padded)
        saved = mixing(
            padded,
            kernels[layer_index],
            gains[layer_index],
            up_weights[layer_index],
            tile_rows,
            tile_cols,
        )
        saved_list.append(saved)
        branch = jnp.dot(
            saved[3], down_weights[layer_index], preferred_element_type=jnp.float32
        ).reshape(tile_rows, tile_cols, channels)
        current = (current.astype(jnp.float32) + branch).astype(jnp.bfloat16)
    gradient = cotangent
    kernel_list = [None] * layer_count
    gain_list = [None] * layer_count
    up_list = [None] * layer_count
    down_list = [None] * layer_count
    for layer_index in reversed(range(layer_count)):
        padded = stored[layer_index]
        saved = saved_list[layer_index]
        conv_grad, kernel_term, gain_term, up_term, down_term = backward_rows(
            padded,
            gradient,
            saved,
            kernels[layer_index],
            gains[layer_index],
            up_weights[layer_index],
            down_weights[layer_index],
            tile_rows,
            tile_cols,
        )
        kernel_list[layer_index] = kernel_term * factor
        gain_list[layer_index] = gain_term * factor
        up_list[layer_index], down_list[layer_index] = deliver(up_term * factor, down_term * factor)
        padded_grad = extended(conv_grad, (("row", 0), ("col", 1)), halo_width)
        gradient = (
            gradient.astype(jnp.float32)
            + flipped_conv(padded_grad, kernels[layer_index], tile_rows, tile_cols)
        ).astype(jnp.bfloat16)
    kernel_total, gain_total = lax.psum(
        (jnp.stack(kernel_list), jnp.stack(gain_list)), ("row", "col")
    )
    return (current, gradient, kernel_total, gain_total, jnp.stack(up_list), jnp.stack(down_list))


def solution(mesh):
    placed = (P("row", "col", None), P(), P(), P(), P(), P("row", "col", None))
    return jax.shard_map(
        per_device,
        mesh=mesh,
        in_specs=placed,
        out_specs=(
            P("row", "col", None),
            P("row", "col", None),
            P(),
            P(),
            P(None, "row", "col"),
            P(None, "col", "row"),
        ),
        check_vma=False,
    )
```

profile of v0, /device:TPU:1, one launch (start us, length us, event | category | flops | bytes accessed | tf_op | source)
XLA Modules:
  0.0 420.7 jit_solution(7900358934226821909)
XLA Ops:
  1.5 3.9 collective-permute-start
  10.3 4.0 collective-permute-start.3
  14.3 3.4 collective-permute-start.2
  18.8 3.9 fusion.242
  27.1 4.0 collective-permute-start.4
  34.3 5.4 %collective-permute-start.6 = (bf16[22,3,96]{2,1,0:T(4,128)(2,1)S(1)}, bf16[22,3,96]{2,1,0:T(4,128)(2,1)S(1)}, u32[]{:S(2)}, u32[]{:S(2)}) collective-permute-start(bf16[22,3,96]{2,1,0:T(4,128)(2,1)S(1)} %get-tuple-element.152), channel_id=1, source_target_pairs={{0,1},{1,2},{2,3},{3,4},{4,5},{5,6},{6,7},{7,8},{8,9},{9,10},{10,1... | collective-permute-start | bytes 38024 | tf_op jit(solution)/shard_map/ppermute | solution.py:20
  42.6 4.3 %fusion.241 = (f32[16,64]{1,0:T(8,128)S(1)}, f32[16,64,96]{2,1,0:T(8,128)S(1)}) fusion(f32[96]{0:T(128)} %get-tuple-element.167, f32[22,70,96]{2,1,0:T(8,128)S(1)} %maximum_convert_fusion.1, f32[96]{0:T(128)} %get-tuple-element.168, f32[96]{0:T(128)} %get-tuple-element.169, f32[96]{0:T(128)} %get-tuple-element.170, f32[96]{0:T(128)} %get-tuple-element.171, ...), kind=kLoop, calls=%fused_computation.616 | loop fusion | flops 9632768 | bytes 19683712 | tf_op jit(solution)/shard_map/reduce_sum | solution.py:87
  50.3 2.5 fusion.118
  59.9 7.1 %collective-permute-start.8 = (bf16[3,64,96]{2,1,0:T(8,128)(2,1)}, bf16[3,64,96]{2,1,0:T(8,128)(2,1)S(1)}, u32[]{:S(2)}, u32[]{:S(2)}) collective-permute-start(bf16[3,64,96]{2,1,0:T(8,128)(2,1)} %get-tuple-element.158), channel_id=1, source_target_pairs={{0,32},{32,64},{64,96},{96,128},{128,160},{160,192},{192,224},{1,3... | collective-permute-start | bytes 110600 | tf_op jit(solution)/shard_map/ppermute | solution.py:20
  74.1 3.9 collective-permute-start.10
  79.2 4.6 %fusion.172 = bf16[16,64,96]{2,1,0:T(8,128)(2,1)S(1)} fusion(f32[22,70,96]{2,1,0:T(8,128)S(1)} %maximum_convert_fusion.2, bf16[16,64,96]{2,1,0:T(8,128)(2,1)S(1)} %copy-done.2, f32[96]{0:T(128)} %get-tuple-element.167, f32[96]{0:T(128)} %get-tuple-element.168, f32[96]{0:T(128)} %get-tuple-element.169, f32[96]{0:T(128)} %get-tuple-element.170, ...), kind=kLoop, calls=%fused_computation.328 | loop fusion | flops 9830400 | bytes 19679616 | tf_op jit(solution)/shard_map/convert_element_type | solution.py:202
  90.4 41.5 %fusion.240 = (bf16[16,384]{1,0:T(8,128)(2,1)S(1)}, bf16[16,384]{1,0:T(8,128)(2,1)S(1)}, bf16[384,16]{0,1:T(8,128)(2,1)S(1)}, bf16[384,16]{0,1:T(8,128)(2,1)S(1)}) fusion(bf16[96,384]{1,0:T(8,128)(2,1)S(1)} %fusion.19, bf16[96,384]{1,0:T(8,128)(2,1)S(1)} %fusion.18, bf16[384,96]{0,1:T(8,128)(2,1)S(1)} %fusion.21, bf16[384,96]{0,1:T(8,128)(2,1)S(1)} %fusion.20), kind=kCustom, calls=%all-reduce-scatter.4 | all-reduce-scatter fusion | flops 196609 | bytes 345088
  133.6 6.4 %collective-permute-start.16 = (bf16[16,384]{1,0:T(8,128)(2,1)S(1)}, bf16[16,384]{1,0:T(8,128)(2,1)S(1)}, u32[]{:S(2)}, u32[]{:S(2)}) collective-permute-start(bf16[16,384]{1,0:T(8,128)(2,1)S(1)} %get-tuple-element.139), channel_id=1, source_target_pairs={{0,32},{32,64},{64,96},{96,128},{128,160},{160,192},{192,224},{1,3... | collective-permute-start | bytes 36872
  140.0 4.6 %collective-permute-start.22 = (bf16[384,16]{0,1:T(8,128)(2,1)S(1)}, bf16[384,16]{0,1:T(8,128)(2,1)S(1)}, u32[]{:S(2)}, u32[]{:S(2)}) collective-permute-start(bf16[384,16]{0,1:T(8,128)(2,1)S(1)} %get-tuple-element.140), channel_id=1, source_target_pairs={{0,32},{32,64},{64,96},{96,128},{128,160},{160,192},{192,224},{1,3... | collective-permute-start | bytes 36872
  144.6 9.7 %collective-permute-start.20 = (bf16[384,16]{0,1:T(8,128)(2,1)S(1)}, bf16[384,16]{0,1:T(8,128)(2,1)S(1)}, u32[]{:S(2)}, u32[]{:S(2)}) collective-permute-start(bf16[384,16]{0,1:T(8,128)(2,1)S(1)} %get-tuple-element.141), channel_id=1, source_target_pairs={{0,32},{32,64},{64,96},{96,128},{128,160},{160,192},{192,224},{1,3... | collective-permute-start | bytes 36872
  154.6 2.3 collective-permute-start.19
  157.6 86.1 %all-reduce.12 = (f32[2,7,7,96]{3,2,1,0:T(8,128)S(1)}, f32[2,96]{1,0:T(2,128)}) all-reduce(f32[2,7,7,96]{3,2,1,0:T(8,128)S(1)} %pad_maximum_fusion, f32[2,96]{1,0:T(2,128)S(1)} %pad_maximum_fusion.10), channel_id=1, replica_groups=mesh['row'=8,'col'=32] {'row','col'}, use_global_device_ids=true, to_apply=%region_106.0 | all-reduce | flops 9600 | bytes 76800 | tf_op jit(solution)/shard_map/psum | solution.py:203
  245.6 3.7 collective-permute-start.17
  250.1 2.7 collective-permute-start.12
  252.9 8.0 %collective-permute-start.23 = (bf16[384,12]{0,1:T(8,128)(2,1)S(1)}, bf16[384,12]{0,1:T(8,128)(2,1)S(1)}, u32[]{:S(2)}, u32[]{:S(2)}) collective-permute-start(bf16[384,12]{0,1:T(8,128)(2,1)S(1)} %slice.1781), channel_id=1, source_target_pairs={{0,64},{32,96},{64,128},{96,160},{128,192},{160,224},{1,65},{33,97... | collective-permute-start | bytes 27656
  261.7 9.9 %collective-permute-start.21 = (bf16[384,12]{0,1:T(8,128)(2,1)S(1)}, bf16[384,12]{0,1:T(8,128)(2,1)S(1)}, u32[]{:S(2)}, u32[]{:S(2)}) collective-permute-start(bf16[384,12]{0,1:T(8,128)(2,1)S(1)} %slice.1780), channel_id=1, source_target_pairs={{0,64},{32,96},{64,128},{96,160},{128,192},{160,224},{1,65},{33,97... | collective-permute-start | bytes 27656
  272.8 131.2 %all-reduce.13 = (bf16[12,384]{1,0:T(8,128)(2,1)S(1)}, bf16[12,384]{1,0:T(8,128)(2,1)S(1)}, bf16[384,12]{0,1:T(8,128)(2,1)S(1)}, bf16[384,12]{0,1:T(8,128)(2,1)S(1)}) all-reduce(bf16[12,384]{1,0:T(8,128)(2,1)S(1)} %constant_dynamic-slice_fusion.2, ...), channel_id=5, replica_groups=mesh['row'=8,'col'=32] {'col'}, use_global_device_ids=true, to_apply=%region_113.0.clone | all-reduce | flops 18432 | bytes 73728
  404.4 8.1 %collective-permute-start.15 = (bf16[22,3,96]{2,1,0:T(4,128)(2,1)S(1)}, bf16[22,3,96]{2,1,0:T(4,128)(2,1)S(1)}, u32[]{:S(2)}, u32[]{:S(2)}) collective-permute-start(bf16[22,3,96]{2,1,0:T(4,128)(2,1)S(1)} %get-tuple-element.149), channel_id=1, source_target_pairs={{1,0},{2,1},{3,2},{4,3},{5,4},{6,5},{7,6},{8,7},{9,8},{10,9},{11,1... | collective-permute-start | bytes 38024 | tf_op jit(solution)/shard_map/ppermute | solution.py:21
  416.3 4.5 %fusion.122 = bf16[16,64,96]{2,1,0:T(8,128)(2,1)} fusion(f32[22,70,96]{2,1,0:T(8,128)S(1)} %maximum_convert_fusion.3, bf16[16,64,96]{2,1,0:T(8,128)(2,1)S(1)} %fusion.172, f32[96]{0:T(128)S(1)} %get-tuple-element.216, f32[96]{0:T(128)S(1)} %get-tuple-element.217, f32[96]{0:T(128)S(1)} %get-tuple-element.218, f32[96]{0:T(128)S(1)} %get-tuple-element.219, ...), kind=kLoop, calls=%fused_computation.229 | loop fusion | flops 9830400 | bytes 19679616 | tf_op jit(solution)/shard_map/convert_element_type | solution.py:202
  (380 shorter events, 50.5 us)
Async XLA Ops:
  1.5 7.3 %collective-permute-start = (bf16[3,64,96]{2,1,0:T(8,128)(2,1)S(1)}, bf16[3,64,96]{2,1,0:T(8,128)(2,1)S(1)}, u32[]{:S(2)}, u32[]{:S(2)}) collective-permute-start(bf16[3,64,96]{2,1,0:T(8,128)(2,1)S(1)} %get-tuple-element.163), channel_id=1, source_target_pairs={{0,32},{32,64},{64,96},{96,128},{128,160},{160,192},{192,224},{1,3... | collective-permute-start | bytes 110600 | tf_op jit(solution)/shard_map/ppermute | solution.py:20
  5.4 4.8 %collective-permute-start.1 = (bf16[3,64,96]{2,1,0:T(8,128)(2,1)S(1)}, bf16[3,64,96]{2,1,0:T(8,128)(2,1)S(1)}, u32[]{:S(2)}, u32[]{:S(2)}) collective-permute-start(bf16[3,64,96]{2,1,0:T(8,128)(2,1)S(1)} %get-tuple-element.162), channel_id=1, source_target_pairs={{32,0},{64,32},{96,64},{128,96},{160,128},{192,160},{224,192},{33,... | collective-permute-start | bytes 110600 | tf_op jit(solution)/shard_map/ppermute | solution.py:21
  10.3 8.2 %collective-permute-start.3 = (bf16[22,3,96]{2,1,0:T(4,128)(2,1)S(1)}, bf16[22,3,96]{2,1,0:T(4,128)(2,1)S(1)}, u32[]{:S(2)}, u32[]{:S(2)}) collective-permute-start(bf16[22,3,96]{2,1,0:T(4,128)(2,1)S(1)} %get-tuple-element.155), channel_id=1, source_target_pairs={{1,0},{2,1},{3,2},{4,3},{5,4},{6,5},{7,6},{8,7},{9,8},{10,9},{11,1... | collective-permute-start | bytes 38024 | tf_op jit(solution)/shard_map/ppermute | solution.py:21
  14.3 4.4 %collective-permute-start.2 = (bf16[22,3,96]{2,1,0:T(4,128)(2,1)S(1)}, bf16[22,3,96]{2,1,0:T(4,128)(2,1)S(1)}, u32[]{:S(2)}, u32[]{:S(2)}) collective-permute-start(bf16[22,3,96]{2,1,0:T(4,128)(2,1)S(1)} %get-tuple-element.154), channel_id=1, source_target_pairs={{0,1},{1,2},{2,3},{3,4},{4,5},{5,6},{6,7},{7,8},{8,9},{9,10},{10,1... | collective-permute-start | bytes 38024 | tf_op jit(solution)/shard_map/ppermute | solution.py:20
  25.8 5.5 %collective-permute-start.5 = (bf16[3,64,96]{2,1,0:T(8,128)(2,1)S(1)}, bf16[3,64,96]{2,1,0:T(8,128)(2,1)S(1)}, u32[]{:S(2)}, u32[]{:S(2)}) collective-permute-start(bf16[3,64,96]{2,1,0:T(8,128)(2,1)S(1)} %get-tuple-element.161), channel_id=1, source_target_pairs={{32,0},{64,32},{96,64},{128,96},{160,128},{192,160},{224,192},{33,... | collective-permute-start | bytes 110600 | tf_op jit(solution)/shard_map/ppermute | solution.py:21
  27.1 5.2 %collective-permute-start.4 = (bf16[3,64,96]{2,1,0:T(8,128)(2,1)S(1)}, bf16[3,64,96]{2,1,0:T(8,128)(2,1)S(1)}, u32[]{:S(2)}, u32[]{:S(2)}) collective-permute-start(bf16[3,64,96]{2,1,0:T(8,128)(2,1)S(1)} %get-tuple-element.160), channel_id=1, source_target_pairs={{0,32},{32,64},{64,96},{96,128},{128,160},{160,192},{192,224},{1,3... | collective-permute-start | bytes 110600 | tf_op jit(solution)/shard_map/ppermute | solution.py:20
  32.3 10.1 %collective-permute-start.7 = (bf16[22,3,96]{2,1,0:T(4,128)(2,1)S(1)}, bf16[22,3,96]{2,1,0:T(4,128)(2,1)S(1)}, u32[]{:S(2)}, u32[]{:S(2)}) collective-permute-start(bf16[22,3,96]{2,1,0:T(4,128)(2,1)S(1)} %get-tuple-element.153), channel_id=1, source_target_pairs={{1,0},{2,1},{3,2},{4,3},{5,4},{6,5},{7,6},{8,7},{9,8},{10,9},{11,1... | collective-permute-start | bytes 38024 | tf_op jit(solution)/shard_map/ppermute | solution.py:21
  34.3 8.1 %collective-permute-start.6 = (bf16[22,3,96]{2,1,0:T(4,128)(2,1)S(1)}, bf16[22,3,96]{2,1,0:T(4,128)(2,1)S(1)}, u32[]{:S(2)}, u32[]{:S(2)}) collective-permute-start(bf16[22,3,96]{2,1,0:T(4,128)(2,1)S(1)} %get-tuple-element.152), channel_id=1, source_target_pairs={{0,1},{1,2},{2,3},{3,4},{4,5},{5,6},{6,7},{7,8},{8,9},{9,10},{10,1... | collective-permute-start | bytes 38024 | tf_op jit(solution)/shard_map/ppermute | solution.py:20
  58.6 13.5 %collective-permute-start.9 = (bf16[3,64,96]{2,1,0:T(8,128)(2,1)}, bf16[3,64,96]{2,1,0:T(8,128)(2,1)S(1)}, u32[]{:S(2)}, u32[]{:S(2)}) collective-permute-start(bf16[3,64,96]{2,1,0:T(8,128)(2,1)} %get-tuple-element.159), channel_id=1, source_target_pairs={{32,0},{64,32},{96,64},{128,96},{160,128},{192,160},{224,192},{33,... | collective-permute-start | bytes 110600 | tf_op jit(solution)/shard_map/ppermute | solution.py:21
  59.9 12.2 %collective-permute-start.8 = (bf16[3,64,96]{2,1,0:T(8,128)(2,1)}, bf16[3,64,96]{2,1,0:T(8,128)(2,1)S(1)}, u32[]{:S(2)}, u32[]{:S(2)}) collective-permute-start(bf16[3,64,96]{2,1,0:T(8,128)(2,1)} %get-tuple-element.158), channel_id=1, source_target_pairs={{0,32},{32,64},{64,96},{96,128},{128,160},{160,192},{192,224},{1,3... | collective-permute-start | bytes 110600 | tf_op jit(solution)/shard_map/ppermute | solution.py:20
  72.1 6.9 %collective-permute-start.11 = (bf16[22,3,96]{2,1,0:T(4,128)(2,1)S(1)}, bf16[22,3,96]{2,1,0:T(4,128)(2,1)S(1)}, u32[]{:S(2)}, u32[]{:S(2)}) collective-permute-start(bf16[22,3,96]{2,1,0:T(4,128)(2,1)S(1)} %get-tuple-element.151), channel_id=1, source_target_pairs={{1,0},{2,1},{3,2},{4,3},{5,4},{6,5},{7,6},{8,7},{9,8},{10,9},{11,1... | collective-permute-start | bytes 38024 | tf_op jit(solution)/shard_map/ppermute | solution.py:21
  74.1 5.0 %collective-permute-start.10 = (bf16[22,3,96]{2,1,0:T(4,128)(2,1)S(1)}, bf16[22,3,96]{2,1,0:T(4,128)(2,1)S(1)}, u32[]{:S(2)}, u32[]{:S(2)}) collective-permute-start(bf16[22,3,96]{2,1,0:T(4,128)(2,1)S(1)} %get-tuple-element.150), channel_id=1, source_target_pairs={{0,1},{1,2},{2,3},{3,4},{4,5},{5,6},{6,7},{7,8},{8,9},{9,10},{10,1... | collective-permute-start | bytes 38024 | tf_op jit(solution)/shard_map/ppermute | solution.py:20
  132.3 113.3 %collective-permute-start.18 = (bf16[16,384]{1,0:T(8,128)(2,1)S(1)}, bf16[16,384]{1,0:T(8,128)(2,1)S(1)}, u32[]{:S(2)}, u32[]{:S(2)}) collective-permute-start(bf16[16,384]{1,0:T(8,128)(2,1)S(1)} %get-tuple-element.138), channel_id=1, source_target_pairs={{0,32},{32,64},{64,96},{96,128},{128,160},{160,192},{192,224},{1,3... | collective-permute-start | bytes 36872
  133.6 119.2 %collective-permute-start.16 = (bf16[16,384]{1,0:T(8,128)(2,1)S(1)}, bf16[16,384]{1,0:T(8,128)(2,1)S(1)}, u32[]{:S(2)}, u32[]{:S(2)}) collective-permute-start(bf16[16,384]{1,0:T(8,128)(2,1)S(1)} %get-tuple-element.139), channel_id=1, source_target_pairs={{0,32},{32,64},{64,96},{96,128},{128,160},{160,192},{192,224},{1,3... | collective-permute-start | bytes 36872
  140.0 131.6 %collective-permute-start.22 = (bf16[384,16]{0,1:T(8,128)(2,1)S(1)}, bf16[384,16]{0,1:T(8,128)(2,1)S(1)}, u32[]{:S(2)}, u32[]{:S(2)}) collective-permute-start(bf16[384,16]{0,1:T(8,128)(2,1)S(1)} %get-tuple-element.140), channel_id=1, source_target_pairs={{0,32},{32,64},{64,96},{96,128},{128,160},{160,192},{192,224},{1,3... | collective-permute-start | bytes 36872
  144.6 127.8 %collective-permute-start.20 = (bf16[384,16]{0,1:T(8,128)(2,1)S(1)}, bf16[384,16]{0,1:T(8,128)(2,1)S(1)}, u32[]{:S(2)}, u32[]{:S(2)}) collective-permute-start(bf16[384,16]{0,1:T(8,128)(2,1)S(1)} %get-tuple-element.141), channel_id=1, source_target_pairs={{0,32},{32,64},{64,96},{96,128},{128,160},{160,192},{192,224},{1,3... | collective-permute-start | bytes 36872
  154.6 89.7 %collective-permute-start.19 = (bf16[12,384]{1,0:T(8,128)(2,1)S(1)}, bf16[12,384]{1,0:T(8,128)(2,1)S(1)}, u32[]{:S(2)}, u32[]{:S(2)}) collective-permute-start(bf16[12,384]{1,0:T(8,128)(2,1)S(1)} %slice.1779), channel_id=1, source_target_pairs={{0,64},{32,96},{64,128},{96,160},{128,192},{160,224},{1,65},{33,97... | collective-permute-start | bytes 27656
  244.3 160.1 %collective-permute-start.13 = (bf16[3,64,96]{2,1,0:T(8,128)(2,1)S(1)}, bf16[3,64,96]{2,1,0:T(8,128)(2,1)S(1)}, u32[]{:S(2)}, u32[]{:S(2)}) collective-permute-start(bf16[3,64,96]{2,1,0:T(8,128)(2,1)S(1)} %get-tuple-element.157), channel_id=1, source_target_pairs={{32,0},{64,32},{96,64},{128,96},{160,128},{192,160},{224,192},{33,... | collective-permute-start | bytes 110600 | tf_op jit(solution)/shard_map/ppermute | solution.py:21
  245.6 4.5 %collective-permute-start.17 = (bf16[12,384]{1,0:T(8,128)(2,1)S(1)}, bf16[12,384]{1,0:T(8,128)(2,1)S(1)}, u32[]{:S(2)}, u32[]{:S(2)}) collective-permute-start(bf16[12,384]{1,0:T(8,128)(2,1)S(1)} %slice.1778), channel_id=1, source_target_pairs={{0,64},{32,96},{64,128},{96,160},{128,192},{160,224},{1,65},{33,97... | collective-permute-start | bytes 27656
  250.1 154.2 %collective-permute-start.12 = (bf16[3,64,96]{2,1,0:T(8,128)(2,1)S(1)}, bf16[3,64,96]{2,1,0:T(8,128)(2,1)S(1)}, u32[]{:S(2)}, u32[]{:S(2)}) collective-permute-start(bf16[3,64,96]{2,1,0:T(8,128)(2,1)S(1)} %get-tuple-element.156), channel_id=1, source_target_pairs={{0,32},{32,64},{64,96},{96,128},{128,160},{160,192},{192,224},{1,3... | collective-permute-start | bytes 110600 | tf_op jit(solution)/shard_map/ppermute | solution.py:20
  252.9 8.8 %collective-permute-start.23 = (bf16[384,12]{0,1:T(8,128)(2,1)S(1)}, bf16[384,12]{0,1:T(8,128)(2,1)S(1)}, u32[]{:S(2)}, u32[]{:S(2)}) collective-permute-start(bf16[384,12]{0,1:T(8,128)(2,1)S(1)} %slice.1781), channel_id=1, source_target_pairs={{0,64},{32,96},{64,128},{96,160},{128,192},{160,224},{1,65},{33,97... | collective-permute-start | bytes 27656
  261.7 10.7 %collective-permute-start.21 = (bf16[384,12]{0,1:T(8,128)(2,1)S(1)}, bf16[384,12]{0,1:T(8,128)(2,1)S(1)}, u32[]{:S(2)}, u32[]{:S(2)}) collective-permute-start(bf16[384,12]{0,1:T(8,128)(2,1)S(1)} %slice.1780), channel_id=1, source_target_pairs={{0,64},{32,96},{64,128},{96,160},{128,192},{160,224},{1,65},{33,97... | collective-permute-start | bytes 27656
  404.4 11.3 %collective-permute-start.15 = (bf16[22,3,96]{2,1,0:T(4,128)(2,1)S(1)}, bf16[22,3,96]{2,1,0:T(4,128)(2,1)S(1)}, u32[]{:S(2)}, u32[]{:S(2)}) collective-permute-start(bf16[22,3,96]{2,1,0:T(4,128)(2,1)S(1)} %get-tuple-element.149), channel_id=1, source_target_pairs={{1,0},{2,1},{3,2},{4,3},{5,4},{6,5},{7,6},{8,7},{9,8},{10,9},{11,1... | collective-permute-start | bytes 38024 | tf_op jit(solution)/shard_map/ppermute | solution.py:21
  412.5 3.2 collective-permute-start.14
  (119 other events, 12160.1 us)
where the time goes:
time: 429 us; the launch traced here: 421 us
  blocking collectives  259 us (60%)
  starting transfers between devices  99.4 us (23%)
  other arithmetic  31.2 us (7%)
  local copies, waits for them, and re-layouts  15.8 us (4%)
  matrix products  8.18 us (2%)
  between operations  4.48 us (1%)
    unnamed x2, blocking collectives  173 us
    psum x1, blocking collectives, per_device(): lax.psum((jnp.stack(kernel_list), jnp.stack(gain_list)), ('row', 'col'))  86.1 us
    unnamed x8, starting transfers between devices  45.8 us
    ppermute x8, starting transfers between devices, extended(): before = lax.ppermute(last, axis, up)  32.4 us
    ppermute x8, starting transfers between devices, extended(): after = lax.ppermute(first, axis, down)  21.2 us
    reduce_sum x6, other arithmetic, kernel_grad(): jnp.sum(padded_f[tap_row:tap_row + tile_rows, tap_col:tap_col + tile_cols...  9.94 us
    convert_element_type x2, other arithmetic, per_device(): gradient = (gradient.astype(jnp.float32) + flipped_conv(padded_grad, kern...  9.1 us
  transfers between devices with their start and end apart: 24, of which 6 were waited for; matrix products, arithmetic and copies ran while one was open for 4% of the time, Pallas kernels for 0%

commit v1 on v0

v1 whole, which is shorter than its diff:
```python
import functools
import math

import jax
import jax.numpy as jnp
from jax import lax
from jax.experimental import pallas as pl
from jax.experimental.pallas import tpu as pltpu
from jax.sharding import PartitionSpec as P

f32 = jnp.float32
bf16 = jnp.bfloat16
MESH = pl.DeviceIdType.MESH

epsilon = 1e-06
inv_sqrt_two_pi = 0.3989422804014327
tail_p = 0.275
tail_c = (
    0.11780924948816489,
    0.04211150374007564,
    0.33393224058082305,
    -0.33099335173379324,
    0.45199869046687746,
    -0.11485832782346941,
)

NX, NZH, NY, NZC = 4, 2, 4, 8
TR, TC, CH, FF, LN = 16, 64, 96, 384, 128
PX = TR * TC
ROWV = 14 * 8
PADDED = 22 * ROWV
HALO = 672
GROUP = 16


def dot(a, b, ca, cb):
    return lax.dot_general(a, b, (((ca,), (cb,)), ((), ())), preferred_element_type=f32)


def iota(shape, dim):
    return lax.broadcasted_iota(jnp.int32, shape, dim)


def kernel(
    image, kernels, gains, ups, downs, cot,
    out, gimg, gker, ggain, gup, gdown,
    img_in, cot_in, out_b, gimg_b, k_in, g_in, u_in, d_in,
    x0, x1, g0, g1, kb, gb, ub, db, stage, gradf, conv, unit, inv, normed, hidden, slope, pregrad, gradb,
    lf, rf, hsend, hrecv, wsum, sblk, rblk, sacc, s2blk, r2blk, wa, wb, wc,
    in_sem, out_sem, hs_sem, hr_sem, s1_sem, r1_sem, s2_sem, r2_sem, as_sem, ar_sem, bs_sem, br_sem, cs_sem, cr_sem,
):
    xs = (x0, x1)
    gs = (g0, g1)
    ri = lax.axis_index("row")
    ci = lax.axis_index("col")
    zh, px = ri // NX, ri % NX
    py, zc = ci // NZC, ci % NZC
    nrow, ncol = NX * NZH, NY * NZC

    def peer_a(d):
        ox = (px + d // NY) % NX
        oy = (py + d % NY) % NY
        return ox, oy, (zh * NX + ox, oy * NZC + zc)

    def peer_b(d):
        oh = (zh + d // NZC) % NZH
        oz = (zc + d % NZC) % NZC
        return oh, oz, (oh * NX + px, py * NZC + oz)

    up_r, dn_r = (ri + nrow - 1) % nrow, (ri + 1) % nrow
    lt_c, rt_c = (ci + ncol - 1) % ncol, (ci + 1) % ncol

    loads = [
        pltpu.make_async_copy(src, dst, in_sem.at[i])
        for i, (src, dst) in enumerate(
            ((image, img_in), (kernels, k_in), (gains, g_in), (ups, u_in), (downs, d_in), (cot, cot_in))
        )
    ]
    for load in loads:
        load.start()

    barrier = pltpu.get_barrier_semaphore()
    near = [(up_r, ci), (dn_r, ci), (ri, lt_c), (ri, rt_c), (up_r, lt_c), (up_r, rt_c), (dn_r, lt_c), (dn_r, rt_c)]
    everyone = near + [peer_a(d)[2] for d in range(1, GROUP)] + [peer_b(d)[2] for d in range(1, GROUP)]
    for device in everyone:
        pl.semaphore_signal(barrier, inc=1, device_id=device, device_id_type=MESH)

    stage[...] = jnp.zeros_like(stage)
    gb[...] = jnp.zeros_like(gb)
    ub[...] = jnp.zeros_like(ub)
    db[...] = jnp.zeros_like(db)
    kb[...] = jnp.zeros_like(kb)

    loads[0].wait()
    stage[:, 0:CH] = img_in[...].astype(f32)

    def spread(r, _):
        for j in range(8):
            x0[pl.ds(pl.multiple_of((r + 3) * ROWV + (3 + j) * 8, 8), 8), :] = stage[
                pl.ds(r * TC + j, 8, stride=8), :
            ]
        return 0

    lax.fori_loop(0, TR, spread, 0)

    pl.semaphore_wait(barrier, len(everyone))

    def send_halo(e, x):
        for q in range(3):
            hsend[e, q * 64 : q * 64 + 64] = x[(3 + q) * ROWV + 24 : (3 + q) * ROWV + 88, :].astype(bf16)
            hsend[e, 192 + q * 64 : 256 + q * 64] = x[(16 + q) * ROWV + 24 : (16 + q) * ROWV + 88, :].astype(bf16)
            hsend[e, 384 + q * 16 : 400 + q * 16] = x[
                pl.ds(3 * ROWV + (3 + q) * 8, TR, stride=ROWV), :
            ].astype(bf16)
            hsend[e, 432 + q * 16 : 448 + q * 16] = x[
                pl.ds(3 * ROWV + (8 + q) * 8 + 7, TR, stride=ROWV), :
            ].astype(bf16)
        for source, size, target, device in (
            (0, 192, 192, (up_r, ci)),
            (192, 192, 0, (dn_r, ci)),
            (384, 48, 432, (ri, lt_c)),
            (432, 48, 384, (ri, rt_c)),
            (384, 48, 624, (up_r, lt_c)),
            (432, 48, 576, (up_r, rt_c)),
            (384, 48, 528, (dn_r, lt_c)),
            (432, 48, 480, (dn_r, rt_c)),
        ):
            pltpu.make_async_remote_copy(
                src_ref=hsend.at[e, pl.ds(source, size)],
                dst_ref=hrecv.at[e, pl.ds(target, size)],
                send_sem=hs_sem.at[e],
                recv_sem=hr_sem.at[e],
                device_id=device,
                device_id_type=MESH,
            ).start()

    m_up = jnp.where(ri == 0, 0.0, 1.0).astype(f32)
    m_dn = jnp.where(ri == nrow - 1, 0.0, 1.0).astype(f32)
    m_lt = jnp.where(ci == 0, 0.0, 1.0).astype(f32)
    m_rt = jnp.where(ci == ncol - 1, 0.0, 1.0).astype(f32)
    first = iota((8, LN), 0) == 0
    last = iota((8, LN), 0) == 7

    def fill_halo(e, x):
        pltpu.make_async_copy(hrecv.at[e], hrecv.at[e], hr_sem.at[e]).wait()
        for q in range(3):
            x[q * ROWV + 24 : q * ROWV + 88, :] = hrecv[e, q * 64 : q * 64 + 64].astype(f32) * m_up
            x[(19 + q) * ROWV + 24 : (19 + q) * ROWV + 88, :] = (
                hrecv[e, 192 + q * 64 : 256 + q * 64].astype(f32) * m_dn
            )
            o = q * 24
            for ref, m, mid, upper, lower in ((lf, m_lt, 384, 480, 576), (rf, m_rt, 432, 528, 624)):
                ref[o + 3 : o + 19, :] = hrecv[e, mid + q * 16 : mid + q * 16 + 16].astype(f32) * m
                ref[o : o + 3, :] = hrecv[e, upper + q * 16 : upper + q * 16 + 16].astype(f32)[13:16] * (m * m_up)
                ref[o + 19 : o + 22, :] = hrecv[e, lower + q * 16 : lower + q * 16 + 16].astype(f32)[0:3] * (m * m_dn)

        def row(r, _):
            base = r * ROWV
            for q in range(3):
                v = x[pl.ds(pl.multiple_of(base + (8 + q) * 8, 8), 8), :]
                edge = jnp.broadcast_to(lf[pl.ds(q * 24 + r, 1), :], (8, LN))
                x[pl.ds(pl.multiple_of(base + q * 8, 8), 8), :] = jnp.where(first, edge, pltpu.roll(v, 1, 0))
                v = x[pl.ds(pl.multiple_of(base + (3 + q) * 8, 8), 8), :]
                edge = jnp.broadcast_to(rf[pl.ds(q * 24 + r, 1), :], (8, LN))
                x[pl.ds(pl.multiple_of(base + (11 + q) * 8, 8), 8), :] = jnp.where(last, edge, pltpu.roll(v, 7, 0))
            return 0

        lax.fori_loop(0, 22, row, 0, unroll=2)

    def conv_row(x, layer, r, flip):
        acc = None
        for a in range(7):
            xa = x[pl.ds(pl.multiple_of((r + a) * ROWV, 8), ROWV), :].reshape(14, 8, LN)
            for b in range(7):
                t = a * 8 + b
                tap = (6 - a) * 8 + 6 - b if flip else t
                term = xa[b : b + 8] * kb[layer, tap][None]
                acc = term if acc is None else acc + term
        return acc

    send_halo(0, x0)

    for load in loads[1:]:
        load.wait()
    for layer in range(2):
        gb[layer, 0:1, 0:CH] = g_in[layer : layer + 1, :]
        ub[layer, 0:CH, :] = u_in[layer]
        db[layer, :, 0:CH] = d_in[layer]
        for a in range(7):
            for b in range(7):
                kb[layer, a * 8 + b, :, 0:CH] = jnp.broadcast_to(k_in[layer, a, b : b + 1, :], (8, CH))
    stage[:, 0:CH] = cot_in[...].astype(f32)

    def spread_cot(r, _):
        for j in range(8):
            gradf[pl.ds(pl.multiple_of(r * TC + j * 8, 8), 8), :] = stage[pl.ds(r * TC + j, 8, stride=8), :]
        return 0

    lax.fori_loop(0, TR, spread_cot, 0)
    lane_ok = jnp.where(iota((8, LN), 1) < CH, 1.0, 0.0).astype(f32)[0:1]

    CHUNK = 256
    ROWS = CHUNK // TC

    def forward(layer):
        x = xs[layer]

        def conv_step(r, _):
            conv[pl.ds(pl.multiple_of(r * TC, TC), TC), :] = conv_row(x, layer, r, False).reshape(TC, LN)
            return 0

        lax.fori_loop(0, TR, conv_step, 0)

        def mix(c, _):
            here = pl.ds(pl.multiple_of(c * CHUNK, CHUNK), CHUNK)
            v = conv[here, :]
            mean = jnp.sum(v, axis=1, keepdims=True) * (1.0 / CH)
            centred = (v - mean) * lane_ok
            variance = jnp.sum(centred * centred, axis=1, keepdims=True) * (1.0 / CH)
            inverse = lax.rsqrt(variance + epsilon)
            u = centred * inverse
            unit[layer, here, :] = u
            inv[layer, here, :] = jnp.broadcast_to(inverse, (CHUNK, LN))
            n = (u * gb[layer, 0:1, :]).astype(bf16)
            normed[layer, here, :] = n
            pre = dot(n, ub[layer], 1, 0)
            z = jnp.abs(pre)
            e = jnp.exp(-0.5 * pre * pre)
            t = 1.0 / (1.0 + tail_p * z)
            poly = tail_c[5] * t + tail_c[4]
            for k in (3, 2, 1, 0):
                poly = poly * t + tail_c[k]
            tail = poly * t * e
            cdf = jnp.where(pre >= 0.0, 1.0 - tail, tail)
            h = (pre * cdf).astype(bf16)
            hidden[layer, here, :] = h
            slope[layer, here, :] = cdf + pre * (e * inv_sqrt_two_pi)
            branch = dot(h, db[layer], 1, 0)
            for r in range(ROWS):
                start = (c * ROWS + r + 3) * ROWV + 24
                centre = x[pl.ds(pl.multiple_of(start, 8), TC), :]
                value = (centre + branch[r * TC : r * TC + TC]).astype(bf16).astype(f32)
                if layer == 0:
                    x1[pl.ds(pl.multiple_of(start, 8), TC), :] = value
                else:
                    for j in range(8):
                        stage[pl.ds((c * ROWS + r) * TC + j, 8, stride=8), :] = value[j * 8 : j * 8 + 8]
            return 0

        lax.fori_loop(0, PX // CHUNK, mix, 0)

    fill_halo(0, x0)
    forward(0)
    send_halo(1, x1)
    fill_halo(1, x1)
    forward(1)
    out_b[...] = stage[:, 0:CH].astype(bf16)
    out_copy = pltpu.make_async_copy(out_b, out, out_sem.at[0])
    out_copy.start()

    def backward(layer):
        x, g = xs[layer], gs[layer]

        def mix(c, total):
            here = pl.ds(pl.multiple_of(c * CHUNK, CHUNK), CHUNK)
            gr = gradf[here, :].astype(bf16)
            gradb[here, :] = gr
            pg = (dot(gr, db[layer], 1, 1) * slope[layer, here, :]).astype(bf16)
            pregrad[here, :] = pg
            ng = dot(pg, ub[layer], 1, 1)
            u = unit[layer, here, :]
            gain_rows = jnp.sum((ng * u).reshape(CHUNK // 8, 8, LN), axis=0)
            m = ng * gb[layer, 0:1, :]
            mean_m = jnp.sum(m, axis=1, keepdims=True) * (1.0 / CH)
            mean_mu = jnp.sum(m * u, axis=1, keepdims=True) * (1.0 / CH)
            cg = inv[layer, here, :] * (m - mean_m - u * mean_mu)
            cg = cg.astype(bf16).astype(f32)
            for r in range(ROWS):
                start = (c * ROWS + r + 3) * ROWV + 24
                g[pl.ds(pl.multiple_of(start, 8), TC), :] = cg[r * TC : r * TC + TC]
            return total + gain_rows

        gain = lax.fori_loop(0, PX // CHUNK, mix, jnp.zeros((8, LN), f32))
        send_halo(3 - layer, g)

        up_sum = dot(normed[layer], pregrad[...], 0, 0)
        down_sum = dot(gradb[...], hidden[layer], 0, 0)
        both = jnp.concatenate([up_sum, down_sum], axis=0).astype(bf16)
        o, k = iota((192, 256), 0), iota((192, 256), 1)
        q = (o * 43691) >> 19
        i = o - q * 12
        pick = (k == ((q >> 1) & 1) * 128 + (q & 1) * 48 + (q >> 2) * 12 + i).astype(f32).astype(bf16)
        rows = dot(pick, both, 1, 0).astype(bf16)
        for y in range(NY):
            k, n = iota((FF, LN), 0), iota((FF, LN), 1)
            pick = ((k == n + y * 96) & (n < 96)).astype(f32).astype(bf16)
            sblk[layer, y] = dot(rows, pick, 1, 0).astype(bf16)
        for d in range(1, GROUP):
            ox, oy, device = peer_a(d)
            pltpu.make_async_remote_copy(
                src_ref=sblk.at[layer, oy, pl.ds(pl.multiple_of(ox * 48, 16), 48)],
                dst_ref=rblk.at[layer, d - 1],
                send_sem=s1_sem.at[layer],
                recv_sem=r1_sem.at[layer],
                device_id=device,
                device_id_type=MESH,
            ).start()

        def tap_row(a, _):
            def add(r, acc):
                xa = x[pl.ds(pl.multiple_of((r + a) * ROWV, 8), ROWV), :].reshape(14, 8, LN)
                gr = g[pl.ds(pl.multiple_of((r + 3) * ROWV + 24, 8), TC), :].reshape(8, 8, LN)
                return tuple(acc[b] + jnp.sum(xa[b : b + 8] * gr, axis=0) for b in range(7))

            acc = lax.fori_loop(0, TR, add, tuple(jnp.zeros((8, LN), f32) for _ in range(7)))
            wsum[pl.ds(pl.multiple_of(a * 64, 64), 56), :] = jnp.concatenate(acc, axis=0)
            return 0

        lax.fori_loop(0, 7, tap_row, 0)
        wsum[56:64, :] = gain
        for a in range(7):
            rows8 = jnp.sum(wsum[a * 64 : a * 64 + 64, :].reshape(8, 8, LN), axis=1)
            wa[layer * 64 + a * 8 : layer * 64 + a * 8 + 8, :] = rows8

    def input_grad(layer):
        g = gs[layer]

        def step(r, _):
            here = pl.ds(pl.multiple_of(r * TC, TC), TC)
            value = gradf[here, :] + conv_row(g, layer, r, True).reshape(TC, LN)
            value = value.astype(bf16).astype(f32)
            if layer == 1:
                gradf[here, :] = value
            else:
                for j in range(8):
                    stage[pl.ds(r * TC + j, 8, stride=8), :] = value[j * 8 : j * 8 + 8]
            return 0

        lax.fori_loop(0, TR, step, 0)

    sacc[...] = jnp.zeros_like(sacc)
    wa[...] = jnp.zeros_like(wa)
    wsum[...] = jnp.zeros_like(wsum)

    def gather_blocks(layer):
        pltpu.make_async_copy(rblk.at[layer], rblk.at[layer], r1_sem.at[layer]).wait()
        total = sblk[layer, py, pl.ds(pl.multiple_of(px * 48, 16), 48)].astype(f32)
        for d in range(1, GROUP):
            total = total + rblk[layer, d - 1].astype(f32)
        sacc[layer * 48 : layer * 48 + 48, :] = total

    backward(1)
    fill_halo(2, g1)
    input_grad(1)
    gather_blocks(1)
    backward(0)

    part = pl.ds(0, (GROUP - 1) * 8)
    mine_a = px * NY + py
    mine_b = zh * NZC + zc
    for d in range(1, GROUP):
        ox, oy, device = peer_a(d)
        pltpu.make_async_remote_copy(
            src_ref=wa.at[pl.ds(pl.multiple_of((ox * NY + oy) * 8, 8), 8)],
            dst_ref=wb.at[0, pl.ds((d - 1) * 8, 8)],
            send_sem=as_sem,
            recv_sem=ar_sem,
            device_id=device,
            device_id_type=MESH,
        ).start()

    fill_halo(3, g0)
    gather_blocks(0)
    o, k = iota((LN, LN), 0), iota((LN, LN), 1)
    pick = ((k == (o >> 4) * 12 + (o & 15)) & ((o & 15) < 12)).astype(f32).astype(bf16)
    s2blk[...] = dot(pick, sacc[...].astype(bf16), 1, 1).astype(bf16)
    for d in range(1, GROUP):
        oh, oz, device = peer_b(d)
        pltpu.make_async_remote_copy(
            src_ref=s2blk.at[pl.ds(pl.multiple_of(oz * 16, 16), 16)],
            dst_ref=r2blk.at[pl.ds((d - 1) * 16, 16)],
            send_sem=s2_sem,
            recv_sem=r2_sem,
            device_id=device,
            device_id_type=MESH,
        ).start()

    pltpu.make_async_copy(wb.at[0, part], wb.at[0, part], ar_sem).wait()
    total = wa[pl.ds(pl.multiple_of(mine_a * 8, 8), 8), :]
    for d in range(1, GROUP):
        total = total + wb[0, (d - 1) * 8 : d * 8, :]
    wb[1, pl.ds(pl.multiple_of(mine_b * 8, 8), 8), :] = total
    for d in range(1, GROUP):
        pltpu.make_async_remote_copy(
            src_ref=wb.at[1, pl.ds(pl.multiple_of(mine_b * 8, 8), 8)],
            dst_ref=wb.at[1, pl.ds(pl.multiple_of(mine_b * 8, 8), 8)],
            send_sem=bs_sem,
            recv_sem=br_sem,
            device_id=peer_b(d)[2],
            device_id_type=MESH,
        ).start()

    input_grad(0)
    gimg_b[...] = stage[:, 0:CH].astype(bf16)
    gimg_copy = pltpu.make_async_copy(gimg_b, gimg, out_sem.at[1])
    gimg_copy.start()

    pltpu.make_async_copy(wb.at[1, part], wb.at[1, part], br_sem).wait()
    total = wb[1, 0:8, :]
    for d in range(1, GROUP):
        total = total + wb[1, d * 8 : d * 8 + 8, :]
    wc[pl.ds(pl.multiple_of(mine_a * 8, 8), 8), :] = total * (1.0 / 512.0)
    for d in range(1, GROUP):
        pltpu.make_async_remote_copy(
            src_ref=wc.at[pl.ds(pl.multiple_of(mine_a * 8, 8), 8)],
            dst_ref=wc.at[pl.ds(pl.multiple_of(mine_a * 8, 8), 8)],
            send_sem=cs_sem,
            recv_sem=cr_sem,
            device_id=peer_a(d)[2],
            device_id_type=MESH,
        ).start()

    pltpu.make_async_copy(r2blk, r2blk, r2_sem).wait()
    total = s2blk[pl.ds(pl.multiple_of(zc * 16, 16), 16), :].astype(f32)
    for d in range(1, GROUP):
        total = total + r2blk[(d - 1) * 16 : d * 16, :].astype(f32)
    total = total * (1.0 / 512.0)
    turned = jnp.concatenate([total, jnp.zeros((LN - 16, LN), f32)], axis=0).T
    for layer in range(2):
        o = layer * 48
        gup[layer] = jnp.where(zh == 0, turned[o : o + 12, 0:12], turned[o + 12 : o + 24, 0:12])
        gdown[layer] = jnp.where(zh == 0, total[0:12, o + 24 : o + 36], total[0:12, o + 36 : o + 48])

    pltpu.make_async_copy(wc.at[part], wc.at[part], cr_sem).wait()
    for layer in range(2):
        for a in range(7):
            gker[layer, a] = wc[layer * 64 + a * 8 : layer * 64 + a * 8 + 7, 0:CH]
        ggain[layer : layer + 1, :] = wc[layer * 64 + 7 : layer * 64 + 8, 0:CH]

    for e in range(4):
        pltpu.make_async_copy(hsend.at[e], hsend.at[e], hs_sem.at[e]).wait()
    for layer in range(2):
        pltpu.make_async_copy(rblk.at[layer], rblk.at[layer], s1_sem.at[layer]).wait()
    pltpu.make_async_copy(r2blk, r2blk, s2_sem).wait()
    pltpu.make_async_copy(wb.at[0, part], wb.at[0, part], as_sem).wait()
    pltpu.make_async_copy(wb.at[1, part], wb.at[1, part], bs_sem).wait()
    pltpu.make_async_copy(wc.at[part], wc.at[part], cs_sem).wait()
    out_copy.wait()
    gimg_copy.wait()


def per_device(image, kernels, gains, ups, downs, cot):
    vmem = pltpu.VMEM
    dma = pltpu.SemaphoreType.DMA
    any_spec = pl.BlockSpec(memory_space=pl.ANY)
    vmem_spec = pl.BlockSpec(memory_space=pltpu.VMEM)
    outs = pl.pallas_call(
        kernel,
        out_shape=(
            jax.ShapeDtypeStruct((PX, CH), bf16),
            jax.ShapeDtypeStruct((PX, CH), bf16),
            jax.ShapeDtypeStruct((2, 7, 7, CH), f32),
            jax.ShapeDtypeStruct((2, CH), f32),
            jax.ShapeDtypeStruct((2, 12, 12), f32),
            jax.ShapeDtypeStruct((2, 12, 12), f32),
        ),
        in_specs=[any_spec] * 6,
        out_specs=(any_spec, any_spec, vmem_spec, vmem_spec, vmem_spec, vmem_spec),
        scratch_shapes=[
            vmem((PX, CH), bf16),
            vmem((PX, CH), bf16),
            vmem((PX, CH), bf16),
            vmem((PX, CH), bf16),
            vmem((2, 7, 7, CH), f32),
            vmem((2, CH), f32),
            vmem((2, CH, FF), bf16),
            vmem((2, FF, CH), bf16),
            vmem((PADDED, LN), f32),
            vmem((PADDED, LN), f32),
            vmem((PADDED, LN), f32),
            vmem((PADDED, LN), f32),
            vmem((2, 56, 8, LN), f32),
            vmem((2, 8, LN), f32),
            vmem((2, LN, FF), bf16),
            vmem((2, FF, LN), bf16),
            vmem((PX, LN), f32),
            vmem((PX, LN), f32),
            vmem((PX, LN), f32),
            vmem((2, PX, LN), f32),
            vmem((2, PX, LN), f32),
            vmem((2, PX, LN), bf16),
            vmem((2, PX, FF), bf16),
            vmem((2, PX, FF), f32),
            vmem((PX, FF), bf16),
            vmem((PX, LN), bf16),
            vmem((72, LN), f32),
            vmem((72, LN), f32),
            vmem((4, HALO, LN), bf16),
            vmem((4, HALO, LN), bf16),
            vmem((7 * 64, LN), f32),
            vmem((2, NY, 192, LN), bf16),
            vmem((2, GROUP - 1, 48, LN), bf16),
            vmem((LN, LN), f32),
            vmem((LN, LN), bf16),
            vmem(((GROUP - 1) * 16, LN), bf16),
            vmem((LN, LN), f32),
            vmem((2, LN, LN), f32),
            vmem((LN, LN), f32),
            dma((6,)),
            dma((2,)),
            dma((4,)),
            dma((4,)),
            dma((2,)),
            dma((2,)),
            dma,
            dma,
            dma,
            dma,
            dma,
            dma,
            dma,
            dma,
        ],
        compiler_params=pltpu.CompilerParams(
            collective_id=0, has_side_effects=True, vmem_limit_bytes=48 * 1024 * 1024
        ),
        cost_estimate=pl.CostEstimate(flops=2000000000, bytes_accessed=2000000, transcendentals=1600000),
    )(image.reshape(PX, CH), kernels, gains, ups, downs, cot.reshape(PX, CH))
    return (outs[0].reshape(TR, TC, CH), outs[1].reshape(TR, TC, CH)) + tuple(outs[2:])


def solution(mesh):
    placed = (P("row", "col", None), P(), P(), P(), P(), P("row", "col", None))
    return jax.shard_map(
        per_device,
        mesh=mesh,
        in_specs=placed,
        out_specs=(
            P("row", "col", None),
            P("row", "col", None),
            P(),
            P(),
            P(None, "row", "col"),
            P(None, "col", "row"),
        ),
        check_vma=False,
    )
```

time: 429 us -> 78 us (0.18); the launches traced: 421 us -> 77.8 us
  blocking collectives: 259 us -> 0 us
  starting transfers between devices: 99.4 us -> 0 us
  Pallas kernels: 0 us -> 70.4 us
  other arithmetic: 31.2 us -> 0 us
  local copies, waits for them, and re-layouts: 15.8 us -> 6.75 us
  matrix products: 8.18 us -> 0 us
    unnamed x2 -> x0, blocking collectives: 173 us -> none
    psum x1 -> x0, blocking collectives: 86.1 us -> none  [per_device(): lax.psum((jnp.stack(kernel_list), jnp.stack(gain_list)), ('row', 'col'))]
    pallas_call x0 -> x1, Pallas kernels: none -> 70.4 us  [per_device(): pl.pallas_call(kernel, out_shape=(jax.ShapeDtypeStruct((PX, CH), bf16), j...]
    ppermute x16 -> x0, starting transfers between devices: 53.6 us -> none  [the longest x8 32.4 us: extended(): before = lax.ppermute(last, axis, up)]
    unnamed x8 -> x0, starting transfers between devices: 45.8 us -> none
    reduce_sum x10 -> x0, other arithmetic: 18.9 us -> none  [the longest x6 9.94 us: kernel_grad(): jnp.sum(padded_f[tap_row:tap_row + tile_rows, tap_col:tap_col + tile_cols...]
    convert_element_type x8 -> x0, other arithmetic: 10.3 us -> none  [the longest x2 9.1 us: per_device(): gradient = (gradient.astype(jnp.float32) + flipped_conv(padded_grad, kern...]
    dot_general x12 -> x0, matrix products: 8.18 us -> none  [the longest x4 3.44 us: contract_trailing(): lax.dot_general(left, right, (((1,), (1,)), ((), ())), preferred_element_...]
  transfers between devices with their start and end apart: 24 -> 0, of which waited for: 6 -> 0; matrix products, arithmetic and copies ran while one was open for 4% -> 0% of each run, Pallas kernels for 0% -> 0%
where the time goes in v1:
time: 78 us; the launch traced here: 77.8 us
  Pallas kernels  70.4 us (90%)
  local copies, waits for them, and re-layouts  6.75 us (9%)
    pallas_call x1, Pallas kernels, per_device(): pl.pallas_call(kernel, out_shape=(jax.ShapeDtypeStruct((PX, CH), bf16), j...  70.4 us
    unnamed x16, local copies, waits for them, and re-layouts  6.75 us

profile of v1, /device:TPU:1, one launch (start us, length us, event | category | flops | bytes accessed | tf_op | source)
XLA Modules:
  0.0 77.8 jit_solution(6536681315332050370)
XLA Ops:
  0.6 0.0 copy-start
  0.6 0.9 %copy.12.kernels = f32[2,7,7,96]{3,2,1,0:T(8,128)S(1)} copy(f32[2,7,7,96]{3,0,2,1:T(2,128)} %param.7) | data formatting | bytes 75264 | tf_op args[1]
  1.5 0.0 copy-start.2
  1.5 0.0 copy-start.3
  1.5 1.1 %copy.13.downs = bf16[2,384,96]{2,1,0:T(8,128)(2,1)S(1)} copy(bf16[2,384,96]{1,2,0:T(8,128)(2,1)} %param.10) | data formatting | bytes 294912 | tf_op args[4]
  2.6 0.0 copy-done
  2.6 0.0 copy-done.2
  2.6 0.0 copy-done.3
  2.7 0.0 copy-start.1
  2.7 0.9 %copy-done.1 = bf16[16,64,96]{2,1,0:T(8,128)(2,1)S(1)} copy-done((bf16[16,64,96]{2,1,0:T(8,128)(2,1)S(1)}, bf16[16,64,96]{2,1,0:T(8,128)(2,1)}, u32[]{:S(2)}) %copy-start.1) | copy-done | bytes 196632
  3.6 70.4 %shard_map.109 = (bf16[1024,96]{1,0:T(8,128)(2,1)S(1)}, bf16[1024,96]{1,0:T(8,128)(2,1)S(1)}, f32[2,7,7,96]{3,2,1,0:T(8,128)S(1)}, f32[2,96]{1,0:T(2,128)S(1)}, ...) custom-call(bf16[1024,96]{1,0:T(8,128)(2,1)S(1)} %bitcast.6, f32[2,7,7,96]{3,2,1,0:T(8,128)S(1)} %copy.12.kernels, ...), custom_call_target="tpu_custom_call" | custom-call | flops 2000000000 | bytes 2000000 | tf_op jit(solution)/shard_map/pallas_call | solution.py:457
  74.0 0.6 copy.15
  74.6 0.6 copy.16
  75.2 0.6 copy.14
  75.9 0.7 copy.20
  76.6 0.7 copy.21
  77.3 0.6 copy.22
Async XLA Ops:
  0.6 2.0 %copy-start = (bf16[16,64,96]{2,1,0:T(8,128)(2,1)S(1)}, bf16[16,64,96]{2,1,0:T(8,128)(2,1)}, u32[]{:S(2)}) copy-start(bf16[16,64,96]{2,1,0:T(8,128)(2,1)} %param.6) | copy-start | bytes 589828
  1.5 1.1 %copy-start.2 = (bf16[2,96,384]{2,1,0:T(8,128)(2,1)S(1)}, bf16[2,96,384]{2,1,0:T(8,128)(2,1)}, u32[]{:S(2)}) copy-start(bf16[2,96,384]{2,1,0:T(8,128)(2,1)} %ups.1) | copy-start | bytes 442372
  1.5 1.1 %copy-start.3 = (f32[2,96]{1,0:T(2,128)S(1)}, f32[2,96]{1,0:T(2,128)}, u32[]{:S(2)}) copy-start(f32[2,96]{1,0:T(2,128)} %gains.1) | copy-start | bytes 2308
  2.7 1.0 %copy-start.1 = (bf16[16,64,96]{2,1,0:T(8,128)(2,1)S(1)}, bf16[16,64,96]{2,1,0:T(8,128)(2,1)}, u32[]{:S(2)}) copy-start(bf16[16,64,96]{2,1,0:T(8,128)(2,1)} %param.11) | copy-start | bytes 589828

commit v2 on v1

v2 whole, which is shorter than its diff:
```python
import functools
import math

import jax
import jax.numpy as jnp
from jax import lax
from jax.experimental import pallas as pl
from jax.experimental.pallas import tpu as pltpu
from jax.sharding import PartitionSpec as P

f32 = jnp.float32
bf16 = jnp.bfloat16
MESH = pl.DeviceIdType.MESH

epsilon = 1e-06
inv_sqrt_two_pi = 0.3989422804014327
half_log2e = -0.7213475204444817
tail_p = 0.275
tail_c = (
    0.11780924948816489,
    0.04211150374007564,
    0.33393224058082305,
    -0.33099335173379324,
    0.45199869046687746,
    -0.11485832782346941,
)

NX, NZH, NY, NZC = 4, 2, 4, 8
TR, TC, CH, FF, LN = 16, 64, 96, 384, 128
PX = TR * TC
ROWV = 14 * 8
PADDED = 22 * ROWV
HALO = 544
GROUP = 16


def reciprocal(d):
    return pltpu.reciprocal(d, approx=True)


def dot(a, b, ca, cb):
    return lax.dot_general(a, b, (((ca,), (cb,)), ((), ())), preferred_element_type=f32)


def iota(shape, dim):
    return lax.broadcasted_iota(jnp.int32, shape, dim)


def kernel(
    image, kernels, gains, ups, downs, cot,
    out, gimg, gker, ggain, gup, gdown,
    img_in, cot_in, out_b, gimg_b, k_in, g_in, u_in, d_in,
    x0, x1, g0, g1, kb, gb, ub, db, stage, gradf, conv, unit, inv, normed, hidden, slope, pregrad, gradb,
    lf, rf, corner, hsend, hrecv, gain, wsum, sblk, rblk, sacc, s2blk, r2blk, wa, wpair, wgroup, wline, wall,
    in_sem, out_sem, hs_sem, hc_sem, hr_sem, s1_sem, r1_sem, s2_sem, r2_sem, ps_sem, pr_sem, as_sem, ar_sem,
    zs_sem, zr_sem, cs_sem, cr_sem,
):
    xs = (x0, x1)
    gs = (g0, g1)
    ri = lax.axis_index("row")
    ci = lax.axis_index("col")
    zh, px = ri // NX, ri % NX
    py, zc = ci // NZC, ci % NZC
    core = ci % 2
    nrow, ncol = NX * NZH, NY * NZC

    def peer_a(d):
        ox = (px + d // NY) % NX
        oy = (py + d % NY) % NY
        return ox, oy, (zh * NX + ox, oy * NZC + zc)

    def peer_b(d):
        oh = (zh + d // NZC) % NZH
        oz = (zc + d % NZC) % NZC
        return oz, (oh * NX + px, py * NZC + oz)

    def send(src, dst, send_sem, recv_sem, device):
        pltpu.make_async_remote_copy(
            src_ref=src, dst_ref=dst, send_sem=send_sem, recv_sem=recv_sem, device_id=device, device_id_type=MESH
        ).start()

    def await_bytes(ref, sem):
        pltpu.make_async_copy(ref, ref, sem).wait()

    up_r, dn_r = (ri + nrow - 1) % nrow, (ri + 1) % nrow
    lt_c, rt_c = (ci + ncol - 1) % ncol, (ci + 1) % ncol
    pair = (ri, ci + 1 - 2 * core)

    loads = [
        pltpu.make_async_copy(src, dst, in_sem.at[i])
        for i, (src, dst) in enumerate(
            ((image, img_in), (kernels, k_in), (gains, g_in), (ups, u_in), (downs, d_in), (cot, cot_in))
        )
    ]
    for load in loads:
        load.start()

    barrier = pltpu.get_barrier_semaphore()
    near = [(up_r, ci), (dn_r, ci), (ri, lt_c), (ri, rt_c), (up_r, lt_c), (up_r, rt_c), (dn_r, lt_c), (dn_r, rt_c)]
    everyone = near + [peer_a(d)[2] for d in range(1, GROUP)] + [peer_b(d)[1] for d in range(1, GROUP)]
    for device in everyone:
        pl.semaphore_signal(barrier, inc=1, device_id=device, device_id_type=MESH)

    def rows(start, size):
        return pl.ds(pl.multiple_of(start, 8), size)

    def pack_halo(e, x):
        for q in range(3):
            left, right = (3 + q) * 8, (8 + q) * 8 + 7
            hsend[e, q * 16 : q * 16 + 16] = x[pl.ds(3 * ROWV + left, TR, stride=ROWV), :].astype(bf16)
            hsend[e, 48 + q * 16 : 64 + q * 16] = x[pl.ds(3 * ROWV + right, TR, stride=ROWV), :].astype(bf16)
            top, bottom = (3 + q) * ROWV + 24, (16 + q) * ROWV + 24
            hsend[e, 96 + q * 64 : 160 + q * 64] = x[top : top + 64, :].astype(bf16)
            hsend[e, 288 + q * 64 : 352 + q * 64] = x[bottom : bottom + 64, :].astype(bf16)
            for c, start in enumerate(
                (3 * ROWV + left, 3 * ROWV + right, 16 * ROWV + left, 16 * ROWV + right)
            ):
                corner[c * 16 + q * 4 : c * 16 + q * 4 + 3, :] = x[pl.ds(start, 3, stride=ROWV), :]
        hsend[e, 480:544] = corner[...].astype(bf16)

    def start_halo(e):
        for source, size, target, sem, device in (
            (0, 48, 48, hc_sem, (ri, lt_c)),
            (48, 48, 0, hc_sem, (ri, rt_c)),
            (96, 192, 288, hr_sem, (up_r, ci)),
            (288, 192, 96, hr_sem, (dn_r, ci)),
            (480, 16, 528, hr_sem, (up_r, lt_c)),
            (496, 16, 512, hr_sem, (up_r, rt_c)),
            (512, 16, 496, hr_sem, (dn_r, lt_c)),
            (528, 16, 480, hr_sem, (dn_r, rt_c)),
        ):
            send(hsend.at[e, pl.ds(source, size)], hrecv.at[e, pl.ds(target, size)], hs_sem.at[e], sem.at[e], device)

    m_up = jnp.where(ri == 0, 0.0, 1.0).astype(f32)
    m_dn = jnp.where(ri == nrow - 1, 0.0, 1.0).astype(f32)
    m_lt = jnp.where(ci == 0, 0.0, 1.0).astype(f32)
    m_rt = jnp.where(ci == ncol - 1, 0.0, 1.0).astype(f32)
    first = iota((8, LN), 0) == 0
    last = iota((8, LN), 0) == 7

    def extend_row(x, r):
        base = r * ROWV
        for q in range(3):
            v = x[rows(base + (8 + q) * 8, 8), :]
            edge = jnp.broadcast_to(lf[pl.ds(q * 24 + r, 1), :], (8, LN))
            x[rows(base + q * 8, 8), :] = jnp.where(first, edge, pltpu.roll(v, 1, 0))
            v = x[rows(base + (3 + q) * 8, 8), :]
            edge = jnp.broadcast_to(rf[pl.ds(q * 24 + r, 1), :], (8, LN))
            x[rows(base + (11 + q) * 8, 8), :] = jnp.where(last, edge, pltpu.roll(v, 7, 0))

    def fill_cols(e, x):
        await_bytes(hrecv.at[e, pl.ds(0, 96)], hc_sem.at[e])
        for q in range(3):
            lf[q * 24 + 3 : q * 24 + 19, :] = hrecv[e, q * 16 : q * 16 + 16].astype(f32) * m_lt
            rf[q * 24 + 3 : q * 24 + 19, :] = hrecv[e, 48 + q * 16 : 64 + q * 16].astype(f32) * m_rt

        def step(i, _):
            extend_row(x, 3 + 2 * i)
            extend_row(x, 4 + 2 * i)
            return 0

        lax.fori_loop(0, TR // 2, step, 0)

    def fill_rows(e, x):
        await_bytes(hrecv.at[e, pl.ds(96, 448)], hr_sem.at[e])
        corners = hrecv[e, 480:544].astype(f32)
        for q in range(3):
            x[q * ROWV + 24 : q * ROWV + 88, :] = hrecv[e, 96 + q * 64 : 160 + q * 64].astype(f32) * m_up
            x[(19 + q) * ROWV + 24 : (19 + q) * ROWV + 88, :] = (
                hrecv[e, 288 + q * 64 : 352 + q * 64].astype(f32) * m_dn
            )
            o = q * 24
            for c, (ref, m, at) in enumerate(
                ((lf, m_lt * m_up, o), (rf, m_rt * m_up, o), (lf, m_lt * m_dn, o + 19), (rf, m_rt * m_dn, o + 19))
            ):
                ref[at : at + 3, :] = corners[c * 16 + q * 4 : c * 16 + q * 4 + 3] * m

        def step(i, _):
            extend_row(x, i)
            extend_row(x, i + 19)
            return 0

        lax.fori_loop(0, 3, step, 0)

    def conv_rows(x, layer, r, count, flip):
        accs = [None] * count
        for a in range(6 + count):
            xa = x[rows((r + a) * ROWV, ROWV), :].reshape(14, 8, LN)
            for b in range(7):
                for n in range(count):
                    if 0 <= a - n < 7:
                        tap = (6 - a + n) * 8 + 6 - b if flip else (a - n) * 8 + b
                        term = xa[b : b + 8] * kb[layer, tap][None]
                        accs[n] = term if accs[n] is None else accs[n] + term
        return accs

    stage[...] = jnp.zeros_like(stage)
    corner[...] = jnp.zeros_like(corner)
    gb[...] = jnp.zeros_like(gb)
    ub[...] = jnp.zeros_like(ub)
    db[...] = jnp.zeros_like(db)
    kb[...] = jnp.zeros_like(kb)
    gain[...] = jnp.zeros_like(gain)
    sacc[...] = jnp.zeros_like(sacc)
    wsum[...] = jnp.zeros_like(wsum)
    wa[...] = jnp.zeros_like(wa)

    loads[0].wait()
    stage[:, 0:CH] = img_in[...].astype(f32)

    def spread(r, _):
        for j in range(8):
            x0[rows((r + 3) * ROWV + (3 + j) * 8, 8), :] = stage[pl.ds(r * TC + j, 8, stride=8), :]
        return 0

    lax.fori_loop(0, TR, spread, 0)
    pack_halo(0, x0)
    for load in loads[1:]:
        load.wait()
    for layer in range(2):
        gb[layer, 0:1, 0:CH] = g_in[layer : layer + 1, :]
        ub[layer, 0:CH, :] = u_in[layer]
        db[layer, 0:CH, :] = d_in[layer]
        for a in range(7):
            for b in range(7):
                kb[layer, a * 8 + b, :, 0:CH] = jnp.broadcast_to(k_in[a, b, layer : layer + 1, :], (8, CH))
    stage[:, 0:CH] = cot_in[...].astype(f32)

    def spread_cot(r, _):
        for j in range(8):
            gradf[rows(r * TC + j * 8, 8), :] = stage[pl.ds(r * TC + j, 8, stride=8), :]
        return 0

    lax.fori_loop(0, TR, spread_cot, 0)
    lane_ok = jnp.where(iota((8, LN), 1) < CH, 1.0, 0.0).astype(f32)[0:1]

    pl.semaphore_wait(barrier, len(everyone))
    start_halo(0)

    def each(inner, conv_step, mix_step):
        if inner:
            if conv_step is not None:
                lax.fori_loop(0, 5, lambda i, c: (conv_step(3 + 2 * i, 2), c)[1], 0)
            if mix_step is not None:
                lax.fori_loop(0, 2, lambda i, c: (mix_step(3 + 5 * i, 5), c)[1], 0)
        else:
            if conv_step is not None:
                lax.fori_loop(0, 2, lambda i, c: (conv_step(13 * i, 3), c)[1], 0)
            if mix_step is not None:
                lax.fori_loop(0, 2, lambda i, c: (mix_step(13 * i, 3), c)[1], 0)

    def forward(layer, inner):
        x = xs[layer]

        def conv_step(r, count):
            for n, acc in enumerate(conv_rows(x, layer, r, count, False)):
                conv[rows((r + n) * TC, TC), :] = acc.reshape(TC, LN)

        def mix(r, count):
            here = pl.ds(pl.multiple_of(r * TC, TC), count * TC)
            v = conv[here, :]
            mean = jnp.sum(v, axis=1, keepdims=True) * (1.0 / CH)
            centred = (v - mean) * lane_ok
            variance = jnp.sum(centred * centred, axis=1, keepdims=True) * (1.0 / CH)
            inverse = lax.rsqrt(variance + epsilon)
            u = centred * inverse
            unit[layer, here, :] = u
            inv[layer, here, :] = jnp.broadcast_to(inverse, (count * TC, LN))
            n = (u * gb[layer, 0:1, :]).astype(bf16)
            normed[layer, here, :] = n
            pre = dot(n, ub[layer], 1, 0)
            e = jnp.exp2(pre * pre * half_log2e)
            t = reciprocal(1.0 + tail_p * jnp.abs(pre))
            poly = tail_c[5] * t + tail_c[4]
            for k in (3, 2, 1, 0):
                poly = poly * t + tail_c[k]
            tail = poly * (t * e)
            cdf = jnp.where(pre >= 0.0, 1.0 - tail, tail)
            h = (pre * cdf).astype(bf16)
            hidden[layer, here, :] = h
            slope[layer, here, :] = cdf + pre * (e * inv_sqrt_two_pi)
            branch = dot(h, db[layer], 1, 1)
            for n in range(count):
                start = (r + n + 3) * ROWV + 24
                value = (x[rows(start, TC), :] + branch[n * TC : n * TC + TC]).astype(bf16).astype(f32)
                if layer == 0:
                    x1[rows(start, TC), :] = value
                else:
                    for j in range(8):
                        stage[pl.ds((r + n) * TC + j, 8, stride=8), :] = value[j * 8 : j * 8 + 8]

        each(inner, conv_step, mix)

    def backward(layer, inner):
        g = gs[layer]

        def mix(r, count):
            here = pl.ds(pl.multiple_of(r * TC, TC), count * TC)
            gr = gradf[here, :].astype(bf16)
            gradb[here, :] = gr
            pg = (dot(gr, db[layer], 1, 0) * slope[layer, here, :]).astype(bf16)
            pregrad[here, :] = pg
            ng = dot(pg, ub[layer], 1, 1)
            u = unit[layer, here, :]
            gain[layer] += jnp.sum((ng * u).reshape(count * 8, 8, LN), axis=0)
            m = ng * gb[layer, 0:1, :]
            mean_m = jnp.sum(m, axis=1, keepdims=True) * (1.0 / CH)
            mean_mu = jnp.sum(m * u, axis=1, keepdims=True) * (1.0 / CH)
            cg = inv[layer, here, :] * (m - mean_m - u * mean_mu)
            cg = cg.astype(bf16).astype(f32)
            for n in range(count):
                g[rows((r + n + 3) * ROWV + 24, TC), :] = cg[n * TC : n * TC + TC]

        each(inner, None, mix)

    def input_grad(layer, inner):
        def step(r, count):
            for n, acc in enumerate(conv_rows(gs[layer], layer, r, count, True)):
                here = rows((r + n) * TC, TC)
                value = (gradf[here, :] + acc.reshape(TC, LN)).astype(bf16).astype(f32)
                if layer == 1:
                    gradf[here, :] = value
                else:
                    for j in range(8):
                        stage[pl.ds((r + n) * TC + j, 8, stride=8), :] = value[j * 8 : j * 8 + 8]

        each(inner, step, None)

    def weight_sums(layer):
        up_sum = dot(normed[layer], pregrad[...], 0, 0)
        down_sum = dot(gradb[...], hidden[layer], 0, 0)
        both = jnp.concatenate([up_sum, down_sum], axis=0).astype(bf16)
        o, k = iota((192, 256), 0), iota((192, 256), 1)
        q = (o * 43691) >> 19
        i = o - q * 12
        pick = (k == ((q >> 1) & 1) * 128 + (q & 1) * 48 + (q >> 2) * 12 + i).astype(f32).astype(bf16)
        ordered = dot(pick, both, 1, 0).astype(bf16)
        for y in range(NY):
            k, n = iota((FF, LN), 0), iota((FF, LN), 1)
            pick = ((k == n + y * 96) & (n < 96)).astype(f32).astype(bf16)
            sblk[layer, y] = dot(ordered, pick, 1, 0).astype(bf16)

    def send_blocks(layer):
        for d in range(1, GROUP):
            ox, oy, device = peer_a(d)
            send(
                sblk.at[layer, oy, pl.ds(pl.multiple_of(ox * 48, 16), 48)],
                rblk.at[layer, d - 1],
                s1_sem.at[layer],
                r1_sem.at[layer],
                device,
            )

    def gather_blocks(layer):
        await_bytes(rblk.at[layer], r1_sem.at[layer])
        total = sblk[layer, py, pl.ds(pl.multiple_of(px * 48, 16), 48)].astype(f32)
        for d in range(1, GROUP):
            total = total + rblk[layer, d - 1].astype(f32)
        sacc[layer * 48 : layer * 48 + 48, :] = total

    def kernel_sums(layer):
        x, g = xs[layer], gs[layer]

        def tap_row(a, _):
            def add(r, acc):
                xa = x[rows((r + a) * ROWV, ROWV), :].reshape(14, 8, LN)
                gr = g[rows((r + 3) * ROWV + 24, TC), :].reshape(8, 8, LN)
                return tuple(acc[b] + jnp.sum(xa[b : b + 8] * gr, axis=0) for b in range(7))

            acc = lax.fori_loop(0, TR, add, tuple(jnp.zeros((8, LN), f32) for _ in range(7)))
            wsum[pl.ds(pl.multiple_of(a * 64, 64), 56), :] = jnp.concatenate(acc, axis=0)
            return 0

        lax.fori_loop(0, 7, tap_row, 0)
        wsum[56:64, :] = gain[layer]
        for a in range(7):
            wa[layer, a * 8 : a * 8 + 8, :] = jnp.sum(wsum[a * 64 : a * 64 + 64, :].reshape(8, 8, LN), axis=1)

    fill_cols(0, x0)
    forward(0, True)
    fill_rows(0, x0)
    forward(0, False)
    pack_halo(1, x1)
    start_halo(1)

    fill_cols(1, x1)
    forward(1, True)
    backward(1, True)
    fill_rows(1, x1)
    forward(1, False)
    backward(1, False)
    pack_halo(2, g1)
    start_halo(2)

    weight_sums(1)
    send_blocks(1)
    kernel_sums(1)
    out_b[...] = stage[:, 0:CH].astype(bf16)
    out_copy = pltpu.make_async_copy(out_b, out, out_sem.at[0])
    out_copy.start()

    fill_cols(2, g1)
    input_grad(1, True)
    backward(0, True)
    fill_rows(2, g1)
    input_grad(1, False)
    backward(0, False)
    pack_halo(3, g0)
    start_halo(3)

    kernel_sums(0)
    send(wa.at[1 - core], wpair, ps_sem, pr_sem, pair)
    weight_sums(0)
    await_bytes(wpair, pr_sem)
    mine_a, mine_z = px * NY + py, zh * (NZC // 2) + zc // 2
    wgroup[mine_a] = (wa[core] + wpair[...]).astype(bf16)
    for d in range(1, GROUP):
        send(wgroup.at[mine_a], wgroup.at[mine_a], as_sem, ar_sem, peer_a(d)[2])
    send_blocks(0)
    gather_blocks(1)

    fill_cols(3, g0)
    input_grad(0, True)
    fill_rows(3, g0)
    input_grad(0, False)

    await_bytes(wgroup.at[pl.ds(0, GROUP - 1)], ar_sem)
    total = wgroup[0].astype(f32)
    for d in range(1, GROUP):
        total = total + wgroup[d].astype(f32)
    wline[mine_z] = total.astype(bf16)
    for d in range(1, 8):
        send(wline.at[mine_z], wline.at[mine_z], zs_sem, zr_sem, peer_b((d // 4) * 8 + (d % 4) * 2)[1])

    gather_blocks(0)
    o, k = iota((LN, LN), 0), iota((LN, LN), 1)
    pick = ((k == (o >> 4) * 12 + (o & 15)) & ((o & 15) < 12)).astype(f32).astype(bf16)
    s2blk[...] = dot(pick, sacc[...].astype(bf16), 1, 1).astype(bf16)
    for d in range(1, GROUP):
        oz, device = peer_b(d)
        send(
            s2blk.at[pl.ds(pl.multiple_of(oz * 16, 16), 16)], r2blk.at[pl.ds((d - 1) * 16, 16)], s2_sem, r2_sem, device
        )

    gimg_b[...] = stage[:, 0:CH].astype(bf16)
    gimg_copy = pltpu.make_async_copy(gimg_b, gimg, out_sem.at[1])
    gimg_copy.start()

    await_bytes(wline.at[pl.ds(0, 7)], zr_sem)
    total = wline[0].astype(f32)
    for d in range(1, 8):
        total = total + wline[d].astype(f32)
    wall[core] = total * (1.0 / 512.0)
    send(wall.at[core], wall.at[core], cs_sem, cr_sem, pair)

    await_bytes(r2blk, r2_sem)
    total = s2blk[pl.ds(pl.multiple_of(zc * 16, 16), 16), :].astype(f32)
    for d in range(1, GROUP):
        total = total + r2blk[(d - 1) * 16 : d * 16, :].astype(f32)
    total = total * (1.0 / 512.0)
    turned = jnp.concatenate([total, jnp.zeros((LN - 16, LN), f32)], axis=0).T
    for layer in range(2):
        o = layer * 48
        gup[:, layer, :] = jnp.where(zh == 0, turned[o : o + 12, 0:12], turned[o + 12 : o + 24, 0:12])
        gdown[:, layer, :] = jnp.where(zh == 0, total[0:12, o + 24 : o + 36], total[0:12, o + 36 : o + 48])

    await_bytes(wall.at[0], cr_sem)
    for layer in range(2):
        for a in range(7):
            gker[a, :, layer, :] = wall[layer, a * 8 : a * 8 + 7, 0:CH]
        ggain[layer : layer + 1, :] = wall[layer, 7:8, 0:CH]

    for e in range(4):
        await_bytes(hsend.at[e], hs_sem.at[e])
    for layer in range(2):
        await_bytes(rblk.at[layer], s1_sem.at[layer])
    await_bytes(r2blk, s2_sem)
    await_bytes(wpair, ps_sem)
    await_bytes(wgroup.at[pl.ds(0, GROUP - 1)], as_sem)
    await_bytes(wline.at[pl.ds(0, 7)], zs_sem)
    await_bytes(wall.at[0], cs_sem)
    out_copy.wait()
    gimg_copy.wait()


def place(*refs):
    for source, target in zip(refs[:6], refs[6:]):
        target[...] = source[...]


def per_device(image, kernels, gains, ups, downs, cot):
    vmem = pltpu.VMEM
    dma = pltpu.SemaphoreType.DMA
    any_spec = pl.BlockSpec(memory_space=pltpu.HBM)
    vmem_spec = pl.BlockSpec(memory_space=pltpu.VMEM)
    outs = pl.pallas_call(
        kernel,
        out_shape=(
            jax.ShapeDtypeStruct((PX, CH), bf16),
            jax.ShapeDtypeStruct((PX, CH), bf16),
            jax.ShapeDtypeStruct((7, 7, 2, CH), f32),
            jax.ShapeDtypeStruct((2, CH), f32),
            jax.ShapeDtypeStruct((12, 2, 12), f32),
            jax.ShapeDtypeStruct((12, 2, 12), f32),
        ),
        in_specs=[any_spec] * 6,
        out_specs=(any_spec, any_spec, vmem_spec, vmem_spec, vmem_spec, vmem_spec),
        scratch_shapes=[
            vmem((PX, CH), bf16),
            vmem((PX, CH), bf16),
            vmem((PX, CH), bf16),
            vmem((PX, CH), bf16),
            vmem((7, 7, 2, CH), f32),
            vmem((2, CH), f32),
            vmem((2, CH, FF), bf16),
            vmem((2, CH, FF), bf16),
            vmem((PADDED, LN), f32),
            vmem((PADDED, LN), f32),
            vmem((PADDED, LN), f32),
            vmem((PADDED, LN), f32),
            vmem((2, 56, 8, LN), f32),
            vmem((2, 8, LN), f32),
            vmem((2, LN, FF), bf16),
            vmem((2, LN, FF), bf16),
            vmem((PX, LN), f32),
            vmem((PX, LN), f32),
            vmem((PX, LN), f32),
            vmem((2, PX, LN), f32),
            vmem((2, PX, LN), f32),
            vmem((2, PX, LN), bf16),
            vmem((2, PX, FF), bf16),
            vmem((2, PX, FF), f32),
            vmem((PX, FF), bf16),
            vmem((PX, LN), bf16),
            vmem((72, LN), f32),
            vmem((72, LN), f32),
            vmem((64, LN), f32),
            vmem((4, HALO, LN), bf16),
            vmem((4, HALO, LN), bf16),
            vmem((2, 8, LN), f32),
            vmem((7 * 64, LN), f32),
            vmem((2, NY, 192, LN), bf16),
            vmem((2, GROUP - 1, 48, LN), bf16),
            vmem((LN, LN), f32),
            vmem((LN, LN), bf16),
            vmem(((GROUP - 1) * 16, LN), bf16),
            vmem((2, 64, LN), f32),
            vmem((64, LN), f32),
            vmem((GROUP, 64, LN), bf16),
            vmem((8, 64, LN), bf16),
            vmem((2, 64, LN), f32),
            dma((6,)),
            dma((2,)),
            dma((4,)),
            dma((4,)),
            dma((4,)),
            dma((2,)),
            dma((2,)),
        ]
        + [dma] * 10,
        compiler_params=pltpu.CompilerParams(
            collective_id=0, has_side_effects=True, vmem_limit_bytes=63 * 1024 * 1024
        ),
        cost_estimate=pl.CostEstimate(flops=2000000000, bytes_accessed=2000000, transcendentals=1600000),
    )(
        image.reshape(PX, CH), kernels.transpose(1, 2, 0, 3), gains, ups, downs.transpose(0, 2, 1), cot.reshape(PX, CH)
    )
    outs = pl.pallas_call(
        place,
        out_shape=tuple(jax.ShapeDtypeStruct(o.shape, o.dtype) for o in outs),
        in_specs=[vmem_spec] * 6,
        out_specs=(vmem_spec,) * 6,
    )(*outs)
    return (
        outs[0].reshape(TR, TC, CH),
        outs[1].reshape(TR, TC, CH),
        outs[2].transpose(2, 0, 1, 3),
        outs[3],
        outs[4].transpose(1, 0, 2),
        outs[5].transpose(1, 0, 2),
    )


def solution(mesh):
    placed = (P("row", "col", None), P(), P(), P(), P(), P("row", "col", None))
    return jax.shard_map(
        per_device,
        mesh=mesh,
        in_specs=placed,
        out_specs=(
            P("row", "col", None),
            P("row", "col", None),
            P(),
            P(),
            P(None, "row", "col"),
            P(None, "col", "row"),
        ),
        check_vma=False,
    )
```

time: 78 us -> 64.3 us (0.82)
  Pallas kernels: 70.4 us -> 63.5 us
  local copies, waits for them, and re-layouts: 6.75 us -> 0 us
    pallas_call x1, Pallas kernels: 70.4 us -> 61.5 us  [per_device(): pl.pallas_call(kernel, out_shape=(jax.ShapeDtypeStruct((PX, CH), bf16), j...]
    unnamed x16 -> x0, local copies, waits for them, and re-layouts: 6.75 us -> none
    pallas_call x0 -> x1, Pallas kernels: none -> 1.96 us  [per_device(): pl.pallas_call(place, out_shape=tuple((jax.ShapeDtypeStruct(o.shape, o.dt...]
where the time goes in v2:
time: 64.3 us; the launch traced here: 64.1 us
  Pallas kernels  63.5 us (99%)
    pallas_call x1, Pallas kernels, per_device(): pl.pallas_call(kernel, out_shape=(jax.ShapeDtypeStruct((PX, CH), bf16), j...  61.5 us
    pallas_call x1, Pallas kernels, per_device(): pl.pallas_call(place, out_shape=tuple((jax.ShapeDtypeStruct(o.shape, o.dt...  1.96 us

profile of v2, /device:TPU:1, one launch (start us, length us, event | category | flops | bytes accessed | tf_op | source)
XLA Modules:
  0.0 64.1 jit_solution(16586659318815943276)
XLA Ops:
  0.6 61.5 %shard_map.109 = (bf16[1024,96]{1,0:T(8,128)(2,1)}, bf16[1024,96]{1,0:T(8,128)(2,1)}, f32[7,7,2,96]{3,2,1,0:T(2,128)}, f32[2,96]{1,0:T(2,128)}, f32[12,2,12]{2,1,0:T(2,128)}, /*index=5*/f32[12,2,12]{2,1,0:T(2,128)}) custom-call(bf16[1024,96]{1,0:T(8,128)(2,1)} %bitcast.9, f32[7,7,2,96]{3,2,1,0:T(2,128)} %bitcast.14, f32[2,96]{1,0:T(2,128)} %gains.1, ...), custom_call_target="tpu_custom_call" | custom-call | flops 2000000000 | bytes 2000000 | tf_op jit(solution)/shard_map/pallas_call | solution.py:496
  62.2 2.0 %shard_map.110 = (bf16[1024,96]{1,0:T(8,128)(2,1)}, bf16[1024,96]{1,0:T(8,128)(2,1)}, f32[7,7,2,96]{3,2,1,0:T(2,128)}, f32[2,96]{1,0:T(2,128)}, f32[12,2,12]{2,1,0:T(2,128)}, /*index=5*/f32[12,2,12]{2,1,0:T(2,128)}) custom-call(bf16[1024,96]{1,0:T(8,128)(2,1)} %get-tuple-element.18.refs_0_, bf16[1024,96]{1,0:T(8,128)(2,1)} %get-tuple-element.19.refs_1_, ...), custom_call_target="tpu_custom_call" | custom-call | tf_op jit(solution)/shard_map/pallas_call | solution.py:568

commit v3 on v2

--- a/solution.py
+++ b/solution.py
@@ -196,6 +196,19 @@
 
     stage[...] = jnp.zeros_like(stage)
     corner[...] = jnp.zeros_like(corner)
+    loads[0].wait()
+    stage[:, 0:CH] = img_in[...].astype(f32)
+
+    def spread(r, _):
+        for j in range(8):
+            x0[rows((r + 3) * ROWV + (3 + j) * 8, 8), :] = stage[pl.ds(r * TC + j, 8, stride=8), :]
+        return 0
+
+    lax.fori_loop(0, TR, spread, 0)
+    pack_halo(0, x0)
+    pl.semaphore_wait(barrier, len(everyone))
+    start_halo(0)
+
     gb[...] = jnp.zeros_like(gb)
     ub[...] = jnp.zeros_like(ub)
     db[...] = jnp.zeros_like(db)
@@ -204,17 +217,6 @@
     sacc[...] = jnp.zeros_like(sacc)
     wsum[...] = jnp.zeros_like(wsum)
     wa[...] = jnp.zeros_like(wa)
-
-    loads[0].wait()
-    stage[:, 0:CH] = img_in[...].astype(f32)
-
-    def spread(r, _):
-        for j in range(8):
-            x0[rows((r + 3) * ROWV + (3 + j) * 8, 8), :] = stage[pl.ds(r * TC + j, 8, stride=8), :]
-        return 0
-
-    lax.fori_loop(0, TR, spread, 0)
-    pack_halo(0, x0)
     for load in loads[1:]:
         load.wait()
     for layer in range(2):
@@ -234,20 +236,29 @@
     lax.fori_loop(0, TR, spread_cot, 0)
     lane_ok = jnp.where(iota((8, LN), 1) < CH, 1.0, 0.0).astype(f32)[0:1]
 
-    pl.semaphore_wait(barrier, len(everyone))
-    start_halo(0)
-
-    def each(inner, conv_step, mix_step):
-        if inner:
-            if conv_step is not None:
+    INNER = ((3, 10),)
+    OUTER = ((0, 3), (13, 3))
+
+    def part(inner, conv_step, mix_step):
+        if conv_step is not None:
+            if inner:
                 lax.fori_loop(0, 5, lambda i, c: (conv_step(3 + 2 * i, 2), c)[1], 0)
-            if mix_step is not None:
-                lax.fori_loop(0, 2, lambda i, c: (mix_step(3 + 5 * i, 5), c)[1], 0)
-        else:
-            if conv_step is not None:
+            else:
                 lax.fori_loop(0, 2, lambda i, c: (conv_step(13 * i, 3), c)[1], 0)
-            if mix_step is not None:
-                lax.fori_loop(0, 2, lambda i, c: (mix_step(13 * i, 3), c)[1], 0)
+        if mix_step is not None:
+            mix_step(INNER if inner else OUTER)
+
+    def take(ref, spans):
+        return jnp.concatenate([ref[r * TC : (r + n) * TC, :] for r, n in spans], axis=0)
+
+    def put(ref, spans, value):
+        at = 0
+        for r, n in spans:
+            ref[r * TC : (r + n) * TC, :] = value[at : at + n * TC]
+            at += n * TC
+
+    def listed(spans):
+        return [r + k for r, n in spans for k in range(n)]
 
     def forward(layer, inner):
         x = xs[layer]
@@ -256,18 +267,17 @@
             for n, acc in enumerate(conv_rows(x, layer, r, count, False)):
                 conv[rows((r + n) * TC, TC), :] = acc.reshape(TC, LN)
 
-        def mix(r, count):
-            here = pl.ds(pl.multiple_of(r * TC, TC), count * TC)
-            v = conv[here, :]
+        def mix(spans):
+            v = take(conv, spans)
             mean = jnp.sum(v, axis=1, keepdims=True) * (1.0 / CH)
             centred = (v - mean) * lane_ok
             variance = jnp.sum(centred * centred, axis=1, keepdims=True) * (1.0 / CH)
             inverse = lax.rsqrt(variance + epsilon)
             u = centred * inverse
-            unit[layer, here, :] = u
-            inv[layer, here, :] = jnp.broadcast_to(inverse, (count * TC, LN))
+            put(unit.at[layer], spans, u)
+            put(inv.at[layer], spans, jnp.broadcast_to(inverse, u.shape))
             n = (u * gb[layer, 0:1, :]).astype(bf16)
-            normed[layer, here, :] = n
+            put(normed.at[layer], spans, n)
             pre = dot(n, ub[layer], 1, 0)
             e = jnp.exp2(pre * pre * half_log2e)
             t = reciprocal(1.0 + tail_p * jnp.abs(pre))
@@ -277,41 +287,41 @@
             tail = poly * (t * e)
             cdf = jnp.where(pre >= 0.0, 1.0 - tail, tail)
             h = (pre * cdf).astype(bf16)
-            hidden[layer, here, :] = h
-            slope[layer, here, :] = cdf + pre * (e * inv_sqrt_two_pi)
+            put(hidden.at[layer], spans, h)
+            put(slope.at[layer], spans, cdf + pre * (e * inv_sqrt_two_pi))
             branch = dot(h, db[layer], 1, 1)
-            for n in range(count):
-                start = (r + n + 3) * ROWV + 24
-                value = (x[rows(start, TC), :] + branch[n * TC : n * TC + TC]).astype(bf16).astype(f32)
+            for n, r in enumerate(listed(spans)):
+                start = (r + 3) * ROWV + 24
+                value = (x[start : start + TC, :] + branch[n * TC : n * TC + TC]).astype(bf16).astype(f32)
                 if layer == 0:
-                    x1[rows(start, TC), :] = value
+                    x1[start : start + TC, :] = value
                 else:
                     for j in range(8):
-                        stage[pl.ds((r + n) * TC + j, 8, stride=8), :] = value[j * 8 : j * 8 + 8]
-
-        each(inner, conv_step, mix)
+                        stage[pl.ds(r * TC + j, 8, stride=8), :] = value[j * 8 : j * 8 + 8]
+
+        part(inner, conv_step, mix)
 
     def backward(layer, inner):
         g = gs[layer]
 
-        def mix(r, count):
-            here = pl.ds(pl.multiple_of(r * TC, TC), count * TC)
-            gr = gradf[here, :].astype(bf16)
-            gradb[here, :] = gr
-            pg = (dot(gr, db[layer], 1, 0) * slope[layer, here, :]).astype(bf16)
-            pregrad[here, :] = pg
+        def mix(spans):
+            gr = take(gradf, spans).astype(bf16)
+            put(gradb, spans, gr)
+            pg = (dot(gr, db[layer], 1, 0) * take(slope.at[layer], spans)).astype(bf16)
+            put(pregrad, spans, pg)
             ng = dot(pg, ub[layer], 1, 1)
-            u = unit[layer, here, :]
-            gain[layer] += jnp.sum((ng * u).reshape(count * 8, 8, LN), axis=0)
+            u = take(unit.at[layer], spans)
+            gain[layer] += jnp.sum((ng * u).reshape(u.shape[0] // 8, 8, LN), axis=0)
             m = ng * gb[layer, 0:1, :]
             mean_m = jnp.sum(m, axis=1, keepdims=True) * (1.0 / CH)
             mean_mu = jnp.sum(m * u, axis=1, keepdims=True) * (1.0 / CH)
-            cg = inv[layer, here, :] * (m - mean_m - u * mean_mu)
+            cg = take(inv.at[layer], spans) * (m - mean_m - u * mean_mu)
             cg = cg.astype(bf16).astype(f32)
-            for n in range(count):
-                g[rows((r + n + 3) * ROWV + 24, TC), :] = cg[n * TC : n * TC + TC]
-
-        each(inner, None, mix)
+            for n, r in enumerate(listed(spans)):
+                start = (r + 3) * ROWV + 24
+                g[start : start + TC, :] = cg[n * TC : n * TC + TC]
+
+        part(inner, None, mix)
 
     def input_grad(layer, inner):
         def step(r, count):
@@ -324,7 +334,7 @@
                     for j in range(8):
                         stage[pl.ds((r + n) * TC + j, 8, stride=8), :] = value[j * 8 : j * 8 + 8]
 
-        each(inner, step, None)
+        part(inner, step, None)
 
     def weight_sums(layer):
         up_sum = dot(normed[layer], pregrad[...], 0, 0)
@@ -358,23 +368,38 @@
             total = total + rblk[layer, d - 1].astype(f32)
         sacc[layer * 48 : layer * 48 + 48, :] = total
 
-    def kernel_sums(layer):
+    def kernel_sums(layer, inner):
         x, g = xs[layer], gs[layer]
 
+        def products(r, a):
+            xa = x[rows((r + a) * ROWV, ROWV), :].reshape(14, 8, LN)
+            gr = g[rows((r + 3) * ROWV + 24, TC), :].reshape(8, 8, LN)
+            return tuple(jnp.sum(xa[b : b + 8] * gr, axis=0) for b in range(7))
+
         def tap_row(a, _):
-            def add(r, acc):
-                xa = x[rows((r + a) * ROWV, ROWV), :].reshape(14, 8, LN)
-                gr = g[rows((r + 3) * ROWV + 24, TC), :].reshape(8, 8, LN)
-                return tuple(acc[b] + jnp.sum(xa[b : b + 8] * gr, axis=0) for b in range(7))
-
-            acc = lax.fori_loop(0, TR, add, tuple(jnp.zeros((8, LN), f32) for _ in range(7)))
-            wsum[pl.ds(pl.multiple_of(a * 64, 64), 56), :] = jnp.concatenate(acc, axis=0)
+            here = pl.ds(pl.multiple_of(a * 64, 64), 56)
+            if inner:
+                zero = tuple(jnp.zeros((8, LN), f32) for _ in range(7))
+                acc = lax.fori_loop(
+                    0, 2, lambda i, acc: fold(acc, [products(3 + 5 * i + n, a) for n in range(5)]), zero
+                )
+                wsum[here, :] = jnp.concatenate(acc, axis=0)
+            else:
+                acc = tuple(wsum[pl.ds(pl.multiple_of(a * 64 + b * 8, 8), 8), :] for b in range(7))
+                acc = fold(acc, [products(r, a) for r in listed(OUTER)])
+                wsum[here, :] = jnp.concatenate(acc, axis=0)
             return 0
 
+        def fold(acc, terms):
+            for term in terms:
+                acc = tuple(p + q for p, q in zip(acc, term))
+            return acc
+
         lax.fori_loop(0, 7, tap_row, 0)
-        wsum[56:64, :] = gain[layer]
-        for a in range(7):
-            wa[layer, a * 8 : a * 8 + 8, :] = jnp.sum(wsum[a * 64 : a * 64 + 64, :].reshape(8, 8, LN), axis=1)
+        if not inner:
+            wsum[56:64, :] = gain[layer]
+            for a in range(7):
+                wa[layer, a * 8 : a * 8 + 8, :] = jnp.sum(wsum[a * 64 : a * 64 + 64, :].reshape(8, 8, LN), axis=1)
 
     fill_cols(0, x0)
     forward(0, True)
@@ -394,7 +419,8 @@
 
     weight_sums(1)
     send_blocks(1)
-    kernel_sums(1)
+    kernel_sums(1, True)
+    kernel_sums(1, False)
     out_b[...] = stage[:, 0:CH].astype(bf16)
     out_copy = pltpu.make_async_copy(out_b, out, out_sem.at[0])
     out_copy.start()
@@ -402,13 +428,14 @@
     fill_cols(2, g1)
     input_grad(1, True)
     backward(0, True)
+    kernel_sums(0, True)
     fill_rows(2, g1)
     input_grad(1, False)
     backward(0, False)
     pack_halo(3, g0)
     start_halo(3)
 
-    kernel_sums(0)
+    kernel_sums(0, False)
     send(wa.at[1 - core], wpair, ps_sem, pr_sem, pair)
     weight_sums(0)
     await_bytes(wpair, pr_sem)

time: 64.3 us -> 59.8 us (0.930)
  Pallas kernels: 63.5 us -> 59 us
    pallas_call x1, Pallas kernels: 61.5 us -> 57 us  [per_device(): pl.pallas_call(kernel, out_shape=(jax.ShapeDtypeStruct((PX, CH), bf16), j...]
where the time goes in v3:
time: 59.8 us; the launch traced here: 59.6 us
  Pallas kernels  59 us (99%)
  between operations  0.64 us (1%)
    pallas_call x1, Pallas kernels, per_device(): pl.pallas_call(kernel, out_shape=(jax.ShapeDtypeStruct((PX, CH), bf16), j...  57 us
    pallas_call x1, Pallas kernels, per_device(): pl.pallas_call(place, out_shape=tuple((jax.ShapeDtypeStruct(o.shape, o.dt...  1.96 us

profile of v3, /device:TPU:1, one launch (start us, length us, event | category | flops | bytes accessed | tf_op | source)
XLA Modules:
  0.0 59.6 jit_solution(9680352100052269715)
XLA Ops:
  0.6 57.0 %shard_map.109 = (bf16[1024,96]{1,0:T(8,128)(2,1)}, bf16[1024,96]{1,0:T(8,128)(2,1)}, f32[7,7,2,96]{3,2,1,0:T(2,128)}, f32[2,96]{1,0:T(2,128)}, f32[12,2,12]{2,1,0:T(2,128)}, /*index=5*/f32[12,2,12]{2,1,0:T(2,128)}) custom-call(bf16[1024,96]{1,0:T(8,128)(2,1)} %bitcast.9, f32[7,7,2,96]{3,2,1,0:T(2,128)} %bitcast.14, f32[2,96]{1,0:T(2,128)} %gains.1, ...), custom_call_target="tpu_custom_call" | custom-call | flops 2000000000 | bytes 2000000 | tf_op jit(solution)/shard_map/pallas_call | solution.py:523
  57.7 2.0 %shard_map.110 = (bf16[1024,96]{1,0:T(8,128)(2,1)}, bf16[1024,96]{1,0:T(8,128)(2,1)}, f32[7,7,2,96]{3,2,1,0:T(2,128)}, f32[2,96]{1,0:T(2,128)}, f32[12,2,12]{2,1,0:T(2,128)}, /*index=5*/f32[12,2,12]{2,1,0:T(2,128)}) custom-call(bf16[1024,96]{1,0:T(8,128)(2,1)} %get-tuple-element.18.refs_0_, bf16[1024,96]{1,0:T(8,128)(2,1)} %get-tuple-element.19.refs_1_, ...), custom_call_target="tpu_custom_call" | custom-call | tf_op jit(solution)/shard_map/pallas_call | solution.py:595

commit v4 on v3

--- a/solution.py
+++ b/solution.py
@@ -51,7 +51,7 @@
     out, gimg, gker, ggain, gup, gdown,
     img_in, cot_in, out_b, gimg_b, k_in, g_in, u_in, d_in,
     x0, x1, g0, g1, kb, gb, ub, db, stage, gradf, conv, unit, inv, normed, hidden, slope, pregrad, gradb,
-    lf, rf, corner, hsend, hrecv, gain, wsum, sblk, rblk, sacc, s2blk, r2blk, wa, wpair, wgroup, wline, wall,
+    lf, rf, corner, hsend, hrecv, gain, pick_rows, pick_cols, pick_units, wsum, sblk, rblk, sacc, s2blk, r2blk, wa, wpair, wgroup, wline, wall,
     in_sem, out_sem, hs_sem, hc_sem, hr_sem, s1_sem, r1_sem, s2_sem, r2_sem, ps_sem, pr_sem, as_sem, ar_sem,
     zs_sem, zr_sem, cs_sem, cr_sem,
 ):
@@ -226,6 +226,15 @@
         for a in range(7):
             for b in range(7):
                 kb[layer, a * 8 + b, :, 0:CH] = jnp.broadcast_to(k_in[a, b, layer : layer + 1, :], (8, CH))
+    o, k = iota((192, 256), 0), iota((192, 256), 1)
+    q = (o * 43691) >> 19
+    i = o - q * 12
+    pick_rows[...] = (k == ((q >> 1) & 1) * 128 + (q & 1) * 48 + (q >> 2) * 12 + i).astype(f32).astype(bf16)
+    for y in range(NY):
+        k, n = iota((FF, LN), 0), iota((FF, LN), 1)
+        pick_cols[y] = ((k == n + y * 96) & (n < 96)).astype(f32).astype(bf16)
+    o, k = iota((LN, LN), 0), iota((LN, LN), 1)
+    pick_units[...] = ((k == (o >> 4) * 12 + (o & 15)) & ((o & 15) < 12)).astype(f32).astype(bf16)
     stage[:, 0:CH] = cot_in[...].astype(f32)
 
     def spread_cot(r, _):
@@ -340,15 +349,9 @@
         up_sum = dot(normed[layer], pregrad[...], 0, 0)
         down_sum = dot(gradb[...], hidden[layer], 0, 0)
         both = jnp.concatenate([up_sum, down_sum], axis=0).astype(bf16)
-        o, k = iota((192, 256), 0), iota((192, 256), 1)
-        q = (o * 43691) >> 19
-        i = o - q * 12
-        pick = (k == ((q >> 1) & 1) * 128 + (q & 1) * 48 + (q >> 2) * 12 + i).astype(f32).astype(bf16)
-        ordered = dot(pick, both, 1, 0).astype(bf16)
+        ordered = dot(pick_rows[...], both, 1, 0).astype(bf16)
         for y in range(NY):
-            k, n = iota((FF, LN), 0), iota((FF, LN), 1)
-            pick = ((k == n + y * 96) & (n < 96)).astype(f32).astype(bf16)
-            sblk[layer, y] = dot(ordered, pick, 1, 0).astype(bf16)
+            sblk[layer, y] = dot(ordered, pick_cols[y], 1, 0).astype(bf16)
 
     def send_blocks(layer):
         for d in range(1, GROUP):
@@ -401,6 +404,38 @@
             for a in range(7):
                 wa[layer, a * 8 : a * 8 + 8, :] = jnp.sum(wsum[a * 64 : a * 64 + 64, :].reshape(8, 8, LN), axis=1)
 
+    mine_a, mine_z = px * NY + py, zh * (NZC // 2) + zc // 2
+    own = pl.ds(pl.multiple_of(core * 32, 32), 32)
+    other = pl.ds(pl.multiple_of(32 - core * 32, 32), 32)
+
+    def pair_send(layer):
+        send(wa.at[layer, other], wpair.at[layer], ps_sem.at[layer], pr_sem.at[layer], pair)
+
+    def group_send(layer):
+        await_bytes(wpair.at[layer], pr_sem.at[layer])
+        wgroup[layer, mine_a] = (wa[layer, own, :] + wpair[layer]).astype(bf16)
+        for d in range(1, GROUP):
+            block = wgroup.at[layer, mine_a]
+            send(block, block, as_sem.at[layer], ar_sem.at[layer], peer_a(d)[2])
+
+    def line_send(layer):
+        await_bytes(wgroup.at[layer, pl.ds(0, GROUP - 1)], ar_sem.at[layer])
+        total = wgroup[layer, 0].astype(f32)
+        for d in range(1, GROUP):
+            total = total + wgroup[layer, d].astype(f32)
+        wline[layer, mine_z] = total.astype(bf16)
+        for d in range(1, 8):
+            block = wline.at[layer, mine_z]
+            send(block, block, zs_sem.at[layer], zr_sem.at[layer], peer_b((d // 4) * 8 + (d % 4) * 2)[1])
+
+    def return_send(layer):
+        await_bytes(wline.at[layer, pl.ds(0, 7)], zr_sem.at[layer])
+        total = wline[layer, 0].astype(f32)
+        for d in range(1, 8):
+            total = total + wline[layer, d].astype(f32)
+        wall[layer, own, :] = total * (1.0 / 512.0)
+        send(wall.at[layer, own], wall.at[layer, own], cs_sem.at[layer], cr_sem.at[layer], pair)
+
     fill_cols(0, x0)
     forward(0, True)
     fill_rows(0, x0)
@@ -421,9 +456,9 @@
     send_blocks(1)
     kernel_sums(1, True)
     kernel_sums(1, False)
-    out_b[...] = stage[:, 0:CH].astype(bf16)
-    out_copy = pltpu.make_async_copy(out_b, out, out_sem.at[0])
-    out_copy.start()
+    pair_send(1)
+    out[...] = stage[:, 0:CH].astype(bf16)
+    group_send(1)
 
     fill_cols(2, g1)
     input_grad(1, True)
@@ -432,53 +467,35 @@
     fill_rows(2, g1)
     input_grad(1, False)
     backward(0, False)
+    kernel_sums(0, False)
+    pair_send(0)
+    weight_sums(0)
+    group_send(0)
+    send_blocks(0)
     pack_halo(3, g0)
     start_halo(3)
-
-    kernel_sums(0, False)
-    send(wa.at[1 - core], wpair, ps_sem, pr_sem, pair)
-    weight_sums(0)
-    await_bytes(wpair, pr_sem)
-    mine_a, mine_z = px * NY + py, zh * (NZC // 2) + zc // 2
-    wgroup[mine_a] = (wa[core] + wpair[...]).astype(bf16)
-    for d in range(1, GROUP):
-        send(wgroup.at[mine_a], wgroup.at[mine_a], as_sem, ar_sem, peer_a(d)[2])
-    send_blocks(0)
+    line_send(1)
     gather_blocks(1)
 
     fill_cols(3, g0)
     input_grad(0, True)
-    fill_rows(3, g0)
-    input_grad(0, False)
-
-    await_bytes(wgroup.at[pl.ds(0, GROUP - 1)], ar_sem)
-    total = wgroup[0].astype(f32)
-    for d in range(1, GROUP):
-        total = total + wgroup[d].astype(f32)
-    wline[mine_z] = total.astype(bf16)
-    for d in range(1, 8):
-        send(wline.at[mine_z], wline.at[mine_z], zs_sem, zr_sem, peer_b((d // 4) * 8 + (d % 4) * 2)[1])
+
+    line_send(0)
 
     gather_blocks(0)
-    o, k = iota((LN, LN), 0), iota((LN, LN), 1)
-    pick = ((k == (o >> 4) * 12 + (o & 15)) & ((o & 15) < 12)).astype(f32).astype(bf16)
-    s2blk[...] = dot(pick, sacc[...].astype(bf16), 1, 1).astype(bf16)
+    s2blk[...] = dot(pick_units[...], sacc[...].astype(bf16), 1, 1).astype(bf16)
     for d in range(1, GROUP):
         oz, device = peer_b(d)
         send(
             s2blk.at[pl.ds(pl.multiple_of(oz * 16, 16), 16)], r2blk.at[pl.ds((d - 1) * 16, 16)], s2_sem, r2_sem, device
         )
 
-    gimg_b[...] = stage[:, 0:CH].astype(bf16)
-    gimg_copy = pltpu.make_async_copy(gimg_b, gimg, out_sem.at[1])
-    gimg_copy.start()
-
-    await_bytes(wline.at[pl.ds(0, 7)], zr_sem)
-    total = wline[0].astype(f32)
-    for d in range(1, 8):
-        total = total + wline[d].astype(f32)
-    wall[core] = total * (1.0 / 512.0)
-    send(wall.at[core], wall.at[core], cs_sem, cr_sem, pair)
+    fill_rows(3, g0)
+    input_grad(0, False)
+    gimg[...] = stage[:, 0:CH].astype(bf16)
+
+    return_send(1)
+    return_send(0)
 
     await_bytes(r2blk, r2_sem)
     total = s2blk[pl.ds(pl.multiple_of(zc * 16, 16), 16), :].astype(f32)
@@ -491,8 +508,8 @@
         gup[:, layer, :] = jnp.where(zh == 0, turned[o : o + 12, 0:12], turned[o + 12 : o + 24, 0:12])
         gdown[:, layer, :] = jnp.where(zh == 0, total[0:12, o + 24 : o + 36], total[0:12, o + 36 : o + 48])
 
-    await_bytes(wall.at[0], cr_sem)
     for layer in range(2):
+        await_bytes(wall.at[layer, pl.ds(0, 32)], cr_sem.at[layer])
         for a in range(7):
             gker[a, :, layer, :] = wall[layer, a * 8 : a * 8 + 7, 0:CH]
         ggain[layer : layer + 1, :] = wall[layer, 7:8, 0:CH]
@@ -502,12 +519,11 @@
     for layer in range(2):
         await_bytes(rblk.at[layer], s1_sem.at[layer])
     await_bytes(r2blk, s2_sem)
-    await_bytes(wpair, ps_sem)
-    await_bytes(wgroup.at[pl.ds(0, GROUP - 1)], as_sem)
-    await_bytes(wline.at[pl.ds(0, 7)], zs_sem)
-    await_bytes(wall.at[0], cs_sem)
-    out_copy.wait()
-    gimg_copy.wait()
+    for layer in range(2):
+        await_bytes(wpair.at[layer], ps_sem.at[layer])
+        await_bytes(wgroup.at[layer, pl.ds(0, GROUP - 1)], as_sem.at[layer])
+        await_bytes(wline.at[layer, pl.ds(0, 7)], zs_sem.at[layer])
+        await_bytes(wall.at[layer, pl.ds(0, 32)], cs_sem.at[layer])
 
 
 def place(*refs):
@@ -523,15 +539,15 @@
     outs = pl.pallas_call(
         kernel,
         out_shape=(
-            jax.ShapeDtypeStruct((PX, CH), bf16),
-            jax.ShapeDtypeStruct((PX, CH), bf16),
-            jax.ShapeDtypeStruct((7, 7, 2, CH), f32),
-            jax.ShapeDtypeStruct((2, CH), f32),
-            jax.ShapeDtypeStruct((12, 2, 12), f32),
-            jax.ShapeDtypeStruct((12, 2, 12), f32),
+            vmem((PX, CH), bf16),
+            vmem((PX, CH), bf16),
+            vmem((7, 7, 2, CH), f32),
+            vmem((2, CH), f32),
+            vmem((12, 2, 12), f32),
+            vmem((12, 2, 12), f32),
         ),
         in_specs=[any_spec] * 6,
-        out_specs=(any_spec, any_spec, vmem_spec, vmem_spec, vmem_spec, vmem_spec),
+        out_specs=(vmem_spec, vmem_spec, vmem_spec, vmem_spec, vmem_spec, vmem_spec),
         scratch_shapes=[
             vmem((PX, CH), bf16),
             vmem((PX, CH), bf16),
@@ -565,6 +581,9 @@
             vmem((4, HALO, LN), bf16),
             vmem((4, HALO, LN), bf16),
             vmem((2, 8, LN), f32),
+            vmem((192, 256), bf16),
+            vmem((NY, FF, LN), bf16),
+            vmem((LN, LN), bf16),
             vmem((7 * 64, LN), f32),
             vmem((2, NY, 192, LN), bf16),
             vmem((2, GROUP - 1, 48, LN), bf16),
@@ -572,9 +591,9 @@
             vmem((LN, LN), bf16),
             vmem(((GROUP - 1) * 16, LN), bf16),
             vmem((2, 64, LN), f32),
-            vmem((64, LN), f32),
-            vmem((GROUP, 64, LN), bf16),
-            vmem((8, 64, LN), bf16),
+            vmem((2, 32, LN), f32),
+            vmem((2, GROUP, 32, LN), bf16),
+            vmem((2, 8, 32, LN), bf16),
             vmem((2, 64, LN), f32),
             dma((6,)),
             dma((2,)),
@@ -583,21 +602,33 @@
             dma((4,)),
             dma((2,)),
             dma((2,)),
+            dma,
+            dma,
         ]
-        + [dma] * 10,
+        + [dma((2,))] * 8,
         compiler_params=pltpu.CompilerParams(
-            collective_id=0, has_side_effects=True, vmem_limit_bytes=63 * 1024 * 1024
+            collective_id=0, has_side_effects=True, vmem_limit_bytes=56 * 1024 * 1024
         ),
         cost_estimate=pl.CostEstimate(flops=2000000000, bytes_accessed=2000000, transcendentals=1600000),
     )(
-        image.reshape(PX, CH), kernels.transpose(1, 2, 0, 3), gains, ups, downs.transpose(0, 2, 1), cot.reshape(PX, CH)
+        *(
+            pltpu.with_memory_space_constraint(array, pltpu.HBM)
+            for array in (
+                image.reshape(PX, CH),
+                kernels.transpose(1, 2, 0, 3),
+                gains,
+                ups,
+                downs.transpose(0, 2, 1),
+                cot.reshape(PX, CH),
+            )
+        )
     )
     outs = pl.pallas_call(
         place,
         out_shape=tuple(jax.ShapeDtypeStruct(o.shape, o.dtype) for o in outs),
         in_specs=[vmem_spec] * 6,
         out_specs=(vmem_spec,) * 6,
-    )(*outs)
+    )(*(pltpu.with_memory_space_constraint(o, pltpu.VMEM) for o in outs))
     return (
         outs[0].reshape(TR, TC, CH),
         outs[1].reshape(TR, TC, CH),

time: 59.8 us -> 55.7 us (0.931)
  Pallas kernels: 59 us -> 54.9 us
    pallas_call x1, Pallas kernels: 57 us -> 54 us  [per_device(): pl.pallas_call(kernel, out_shape=(vmem((PX, CH), bf16), vmem((PX, CH), bf...]
    pallas_call x1, Pallas kernels: 1.96 us -> 0.92 us  [per_device(): pl.pallas_call(place, out_shape=tuple((jax.ShapeDtypeStruct(o.shape, o.dt...]
where the time goes in v4:
time: 55.7 us; the launch traced here: 55.6 us
  Pallas kernels  54.9 us (99%)
  between operations  0.64 us (1%)
    pallas_call x1, Pallas kernels, per_device(): pl.pallas_call(kernel, out_shape=(vmem((PX, CH), bf16), vmem((PX, CH), bf...  54 us

profile of v4, /device:TPU:1, one launch (start us, length us, event | category | flops | bytes accessed | tf_op | source)
XLA Modules:
  0.0 55.6 jit_solution(6722610635423988067)
XLA Ops:
  0.6 54.0 %shard_map.109 = (bf16[1024,96]{1,0:T(8,128)(2,1)S(1)}, bf16[1024,96]{1,0:T(8,128)(2,1)S(1)}, f32[7,7,2,96]{3,2,1,0:T(2,128)S(1)}, f32[2,96]{1,0:T(2,128)S(1)}, ...) custom-call(bf16[1024,96]{1,0:T(8,128)(2,1)} %bitcast.9, f32[7,7,2,96]{3,2,1,0:T(2,128)} %bitcast.14, f32[2,96]{1,0:T(2,128)} %gains.1, ...), custom_call_target="tpu_custom_call" | custom-call | flops 2000000000 | bytes 2000000 | tf_op jit(solution)/shard_map/pallas_call | solution.py:539
  54.6 0.9 %shard_map.110 = (bf16[1024,96]{1,0:T(8,128)(2,1)}, bf16[1024,96]{1,0:T(8,128)(2,1)}, f32[7,7,2,96]{3,2,1,0:T(2,128)}, f32[2,96]{1,0:T(2,128)}, f32[12,2,12]{2,1,0:T(2,128)}, /*index=5*/f32[12,2,12]{2,1,0:T(2,128)}) custom-call(bf16[1024,96]{1,0:T(8,128)(2,1)S(1)} %get-tuple-element.18.refs_0_, bf16[1024,96]{1,0:T(8,128)(2,1)S(1)} %get-tuple-element.19.refs_1_, ...), custom_call_target="tpu_custom_call" | custom-call | tf_op jit(solution)/shard_map/pallas_call | solution.py:626

commit v5 on v4

--- a/solution.py
+++ b/solution.py
@@ -122,12 +122,12 @@
         for source, size, target, sem, device in (
             (0, 48, 48, hc_sem, (ri, lt_c)),
             (48, 48, 0, hc_sem, (ri, rt_c)),
-            (96, 192, 288, hr_sem, (up_r, ci)),
-            (288, 192, 96, hr_sem, (dn_r, ci)),
             (480, 16, 528, hr_sem, (up_r, lt_c)),
             (496, 16, 512, hr_sem, (up_r, rt_c)),
             (512, 16, 496, hr_sem, (dn_r, lt_c)),
             (528, 16, 480, hr_sem, (dn_r, rt_c)),
+            (96, 192, 288, hr_sem, (up_r, ci)),
+            (288, 192, 96, hr_sem, (dn_r, ci)),
         ):
             send(hsend.at[e, pl.ds(source, size)], hrecv.at[e, pl.ds(target, size)], hs_sem.at[e], sem.at[e], device)
 
@@ -268,6 +268,45 @@
 
     def listed(spans):
         return [r + k for r, n in spans for k in range(n)]
+
+    def conv_inside(layer):
+        x = xs[layer]
+        lf[...] = jnp.zeros_like(lf)
+        rf[...] = jnp.zeros_like(rf)
+
+        def extend(i, _):
+            extend_row(x, 3 + 2 * i)
+            extend_row(x, 4 + 2 * i)
+            return 0
+
+        def step(i, _):
+            for n, acc in enumerate(conv_rows(x, layer, 3 + 2 * i, 2, False)):
+                conv[rows((3 + 2 * i + n) * TC, TC), :] = acc.reshape(TC, LN)
+            return 0
+
+        lax.fori_loop(0, TR // 2, extend, 0)
+        lax.fori_loop(0, 5, step, 0)
+
+    def conv_rims(layer):
+        def step(i, _):
+            r = 3 + i
+            sums = [None] * 8
+            for a in range(7):
+                for q in range(3):
+                    edge = jnp.broadcast_to(lf[pl.ds(q * 24 + r + a, 1), :], (8, LN))
+                    for j in range(q + 1):
+                        term = edge * kb[layer, a * 8 + q - j]
+                        sums[j] = term if sums[j] is None else sums[j] + term
+                    edge = jnp.broadcast_to(rf[pl.ds(q * 24 + r + a, 1), :], (8, LN))
+                    for j in range(5 + q, 8):
+                        term = edge * kb[layer, a * 8 + 11 + q - j]
+                        sums[j] = term if sums[j] is None else sums[j] + term
+            for j in range(8):
+                if sums[j] is not None:
+                    conv[rows(r * TC + j * 8, 8), :] += jnp.where(first if j < 3 else last, sums[j], 0.0)
+            return 0
+
+        lax.fori_loop(0, 10, step, 0)
 
     def forward(layer, inner):
         x = xs[layer]
@@ -308,7 +347,9 @@
                     for j in range(8):
                         stage[pl.ds(r * TC + j, 8, stride=8), :] = value[j * 8 : j * 8 + 8]
 
-        part(inner, conv_step, mix)
+        if inner:
+            conv_rims(layer)
+        part(inner, None if inner else conv_step, mix)
 
     def backward(layer, inner):
         g = gs[layer]
@@ -436,6 +477,7 @@
         wall[layer, own, :] = total * (1.0 / 512.0)
         send(wall.at[layer, own], wall.at[layer, own], cs_sem.at[layer], cr_sem.at[layer], pair)
 
+    conv_inside(0)
     fill_cols(0, x0)
     forward(0, True)
     fill_rows(0, x0)
@@ -443,6 +485,7 @@
     pack_halo(1, x1)
     start_halo(1)
 
+    conv_inside(1)
     fill_cols(1, x1)
     forward(1, True)
     backward(1, True)

time: 55.7 us -> 54.8 us (0.984)
  Pallas kernels: 54.9 us -> 54 us
    pallas_call x1, Pallas kernels: 54 us -> 53.1 us  [per_device(): pl.pallas_call(kernel, out_shape=(vmem((PX, CH), bf16), vmem((PX, CH), bf...]
where the time goes in v5:
time: 54.8 us; the launch traced here: 54.7 us
  Pallas kernels  54 us (99%)
  between operations  0.64 us (1%)
    pallas_call x1, Pallas kernels, per_device(): pl.pallas_call(kernel, out_shape=(vmem((PX, CH), bf16), vmem((PX, CH), bf...  53.1 us

profile of v5, /device:TPU:1, one launch (start us, length us, event | category | flops | bytes accessed | tf_op | source)
XLA Modules:
  0.0 54.7 jit_solution(7109059172115488697)
XLA Ops:
  0.6 53.1 %shard_map.109 = (bf16[1024,96]{1,0:T(8,128)(2,1)S(1)}, bf16[1024,96]{1,0:T(8,128)(2,1)S(1)}, f32[7,7,2,96]{3,2,1,0:T(2,128)S(1)}, f32[2,96]{1,0:T(2,128)S(1)}, ...) custom-call(bf16[1024,96]{1,0:T(8,128)(2,1)} %bitcast.9, f32[7,7,2,96]{3,2,1,0:T(2,128)} %bitcast.14, f32[2,96]{1,0:T(2,128)} %gains.1, ...), custom_call_target="tpu_custom_call" | custom-call | flops 2000000000 | bytes 2000000 | tf_op jit(solution)/shard_map/pallas_call | solution.py:582
  53.8 0.9 %shard_map.110 = (bf16[1024,96]{1,0:T(8,128)(2,1)}, bf16[1024,96]{1,0:T(8,128)(2,1)}, f32[7,7,2,96]{3,2,1,0:T(2,128)}, f32[2,96]{1,0:T(2,128)}, f32[12,2,12]{2,1,0:T(2,128)}, /*index=5*/f32[12,2,12]{2,1,0:T(2,128)}) custom-call(bf16[1024,96]{1,0:T(8,128)(2,1)S(1)} %get-tuple-element.18.refs_0_, bf16[1024,96]{1,0:T(8,128)(2,1)S(1)} %get-tuple-element.19.refs_1_, ...), custom_call_target="tpu_custom_call" | custom-call | tf_op jit(solution)/shard_map/pallas_call | solution.py:669
